TPU v7x, 512 devices: a whole 4x4x16 slice. The times are simulated.
512 devices in a mesh: section: 32 (over y, z_lo), tensor: 16 (over z_hi, x, core).
Axes of the slice: x: 4, y: 4, z: 16 (z_hi: 2, z_lo: 8; z = z_hi * 8 + z_lo), core: 2. Of those that a mesh axis runs over, the one named last changes fastest.
Arguments:
- inputs: bfloat16 [4, 64, 8192], P(None, 'section', 'tensor'), may hold values from -6 to 6
- cotangent: bfloat16 [4, 64, 8192], P(None, 'section', 'tensor'), may hold values from -1.5 to 1.5
- plan: int32 [4], replicated, may hold values from 0 to 3, each once
- weights: bfloat16 [32, 1664, 8192], P('section', None, 'tensor'), may hold values from -0.0625 to 0.0625
Outputs:
- grads: bfloat16 [32, 1664, 8192], P('section', None, 'tensor')
Inputs may be any that keep to these rules, and one draw needn't show every extreme that they name: `plan`: a permutation of the 4 micro-batches.
All inputs are finite; a program needn't handle non-finite values.
Results may differ from a plain program's by a relative error of at most 0.028.
Values may be sent and summed in bfloat16 or wider, within the bound.
No kernel may reach another device: no remote copies, remote signals or barrier semaphores. Data moves between devices by JAX's collectives and lax.ppermute only.
A program may use at most 64 MiB of HBM per device.

v0:
```python
import jax
import jax.numpy as jnp
from jax import lax
from jax.sharding import PartitionSpec as P


def swapped(block, axis, bit):
    count = lax.axis_size(axis)
    route = []
    for low in range(count):
        high = low | 1 << bit
        if high != low and high < count:
            route += [(low, high), (high, low)]
    return lax.ppermute(block, axis, route)


def from_behind(value, axis, steps):
    count = lax.axis_size(axis)
    initial, last = (max(0, -steps), min(count, count - steps))
    return lax.ppermute(value, axis, [(source, source + steps) for source in range(initial, last)])


def silu_slope(pre_sum):
    logistic = jax.nn.sigmoid(pre_sum)
    return logistic * (1.0 + pre_sum * (1.0 - logistic))


def local(inputs, cotangent, plan, weights):
    sections = lax.axis_size("section")
    position = lax.axis_index("section")
    copies = sections // 2
    mirror_bit = copies.bit_length() - 1
    lower_section = position < copies
    all_inputs, all_cots = (
        lax.all_gather(inputs, "section", axis=1, tiled=True),
        lax.all_gather(cotangent, "section", axis=1, tiled=True),
    )
    entering = jnp.take(all_inputs, plan, axis=0)
    own_piece = weights[0]
    batches = entering.shape[0]
    row_count = entering.shape[1]
    piece_rows = own_piece.shape[0]
    columns = own_piece.shape[1]
    blank = jnp.zeros((row_count, piece_rows), jnp.float32)

    def project(values):
        return jnp.einsum("rd,fd->rf", values, own_piece, preferred_element_type=jnp.float32)

    def skip_project(values):
        return blank

    def accumulate(left_rows, right_rows, gradient_sum):
        return gradient_sum + jnp.einsum(
            "rf,rd->fd", left_rows, right_rows, preferred_element_type=jnp.float32
        )

    def skip_accumulate(left_rows, right_rows, gradient_sum):
        return gradient_sum

    gradient_sum = jnp.zeros((piece_rows, columns), jnp.float32)
    received = jnp.zeros((row_count, piece_rows), jnp.bfloat16)
    parked = []
    for moment in range(batches + 2):
        back_micro = moment - 2
        mid_micro = moment - 1
        mid_pick = min(max(mid_micro, 0), batches - 1)
        back_pick = min(max(back_micro, 0), batches - 1)
        pre_sum = blank
        outcome = None
        if moment <= batches:
            fwd_pick = min(moment, batches - 1)
            operand = jnp.where(lower_section, entering[fwd_pick], all_cots[mid_pick])
            active = jnp.where(lower_section, moment < batches, mid_micro >= 0)
            product = lax.cond(active, project, skip_project, operand)
            pre_sum = lax.psum(product.astype(jnp.bfloat16), "tensor").astype(jnp.float32)
            outcome = jnp.where(lower_section, jax.nn.silu(pre_sum), pre_sum).astype(jnp.bfloat16)
        parked_slot = parked[back_micro] if back_micro >= 0 else blank
        sending = jnp.where(lower_section, pre_sum, parked_slot)
        returned = swapped(sending.astype(jnp.bfloat16), "section", mirror_bit).astype(
            sending.dtype
        )
        parked.append(returned)
        if moment >= 1:
            grad_pre = (received.astype(jnp.float32) * silu_slope(returned)).astype(jnp.bfloat16)
            left_rows = jnp.where(lower_section, grad_pre, received)
            right_rows = jnp.where(lower_section, entering[back_pick], all_cots[mid_pick])
            active_back = jnp.where(lower_section, back_micro >= 0, mid_micro < batches)
            gradient_sum = lax.cond(
                active_back, accumulate, skip_accumulate, left_rows, right_rows, gradient_sum
            )
        if moment <= batches:
            from_below = from_behind(outcome, "section", copies)
            from_above = from_behind(outcome, "section", -copies)
            received = jnp.where(lower_section, from_above, from_below)
    return gradient_sum.astype(jnp.bfloat16).reshape(1, piece_rows, columns)


def solution(mesh):
    placed = (
        P(None, "section", "tensor"),
        P(None, "section", "tensor"),
        P(),
        P("section", None, "tensor"),
    )
    return jax.shard_map(
        local, mesh=mesh, in_specs=placed, out_specs=P("section", None, "tensor"), check_vma=False
    )
```

profile of v0, /device:TPU:8, one launch (start us, length us, event | category | flops | bytes accessed | tf_op | source)
XLA Modules:
  0.0 619.2 jit_solution(13879255971930831600)
XLA Ops:
  6.5 0.8 compare_select_fusion
  7.3 0.7 compare_and_fusion
  8.0 0.7 copy.9
  8.7 114.9 %all_gather.6 = bf16[4,64,512]{2,0,1:T(4,128)(2,1)S(1)} all-gather(bf16[4,2,512]{2,0,1:T(4,128)(2,1)S(1)} %copy.9), channel_id=1, replica_groups=mesh['section'=32,'tensor'=16] {'section'}, dimensions={1}, use_global_device_ids=true | all-gather | bytes 270336 | tf_op jit(solution)/shard_map/all_gather | solution.py:35
  123.6 0.7 copy.11
  124.3 103.8 %all_gather.7 = bf16[4,64,512]{2,0,1:T(4,128)(2,1)S(1)} all-gather(bf16[4,2,512]{2,0,1:T(4,128)(2,1)S(1)} %copy.11), channel_id=1, replica_groups=mesh['section'=32,'tensor'=16] {'section'}, dimensions={1}, use_global_device_ids=true | all-gather | bytes 270336 | tf_op jit(solution)/shard_map/all_gather | solution.py:36
  228.5 0.6 gather_fusion
  229.2 1.3 convolution_convert_fusion.2
  230.5 1.3 convolution_convert_fusion
  231.8 1.3 convolution_convert_fusion.1
  233.2 0.7 select_bitcast_fusion
  233.9 1.5 conditional.4
  233.9 1.5 fusion.124
  235.4 0.6 copy-done.6
  236.1 277.5 %all-reduce.3.cloned.1.call-done = (bf16[64,1664]{1,0:T(8,128)(2,1)}, bf16[64,1664]{1,0:T(8,128)(2,1)}, bf16[64,1664]{1,0:T(8,128)(2,1)}, bf16[64,1664]{1,0:T(8,128)(2,1)}, bf16[64,1664]{1,0:T(8,128)(2,1)}) async-done(((bf16[64,1664]{1,0:T(8,128)(2,1)}, bf16[64,1664]{1,0:T(8,128)(2,1)}, bf16[64,1664]{1,0:T(8,128)(2,1)}, bf16[64,1664]{1,0:T(8,128)(2,1)}, bf16[64,1664]{1,0:T(8,128)(2,1)}), ...) | async-done | bytes 1064976 | tf_op jit(solution)/shard_map/psum | solution.py:75
  513.7 1.1 fusion.46
  514.8 1.3 collective-permute-start
  516.1 6.1 collective-permute-start.1
  522.2 1.9 collective-permute-start.5
  524.1 1.8 fusion.51
  525.9 1.3 collective-permute-start.3
  527.1 7.4 %collective-permute-start.4 = (bf16[64,1664]{1,0:T(8,128)(2,1)}, bf16[64,1664]{1,0:T(8,128)(2,1)}, u32[]{:S(2)}, u32[]{:S(2)}) collective-permute-start(bf16[64,1664]{1,0:T(8,128)(2,1)} %get-tuple-element.124), channel_id=1, source_target_pairs={{0,256},{16,272},{32,288},{48,304},{64,320},{80,336},{96,352},{112... | collective-permute-start | bytes 638984 | tf_op jit(solution)/shard_map/ppermute | solution.py:20
  534.6 1.9 collective-permute-start.2
  536.5 1.9 fusion.52
  538.3 5.5 collective-permute-done.2
  543.8 1.3 collective-permute-start.7
  545.1 7.4 %collective-permute-start.8 = (bf16[64,1664]{1,0:T(8,128)(2,1)}, bf16[64,1664]{1,0:T(8,128)(2,1)}, u32[]{:S(2)}, u32[]{:S(2)}) collective-permute-start(bf16[64,1664]{1,0:T(8,128)(2,1)} %get-tuple-element.127), channel_id=1, source_target_pairs={{0,256},{16,272},{32,288},{48,304},{64,320},{80,336},{96,352},{112... | collective-permute-start | bytes 638984 | tf_op jit(solution)/shard_map/ppermute | solution.py:20
  552.6 1.9 collective-permute-start.6
  554.5 1.2 fusion.61
  555.7 0.4 conditional.5
  556.1 6.3 %collective-permute-done.6 = bf16[64,1664]{1,0:T(8,128)(2,1)} collective-permute-done((bf16[64,1664]{1,0:T(8,128)(2,1)}, bf16[64,1664]{1,0:T(8,128)(2,1)}, u32[]{:S(2)}, u32[]{:S(2)}) %collective-permute-start.6) | collective-permute-done | bytes 213024 | tf_op jit(solution)/shard_map/ppermute | solution.py:14
  562.4 1.9 collective-permute-start.9
  564.3 1.2 fusion.66
  565.5 7.9 %collective-permute-done.9 = bf16[64,1664]{1,0:T(8,128)(2,1)S(1)} collective-permute-done((bf16[64,1664]{1,0:T(8,128)(2,1)}, bf16[64,1664]{1,0:T(8,128)(2,1)S(1)}, u32[]{:S(2)}, u32[]{:S(2)}) %collective-permute-start.9) | collective-permute-done | bytes 213024 | tf_op jit(solution)/shard_map/ppermute | solution.py:14
  573.4 1.3 collective-permute-start.10
  574.7 6.1 collective-permute-start.11
  580.8 1.4 collective-permute-start.13
  582.2 1.7 fusion.76
  584.0 6.3 %collective-permute-start.14 = (bf16[64,1664]{1,0:T(8,128)(2,1)S(1)}, bf16[64,1664]{1,0:T(8,128)(2,1)S(1)}, u32[]{:S(2)}, u32[]{:S(2)}) collective-permute-start(bf16[64,1664]{1,0:T(8,128)(2,1)S(1)} %get-tuple-element.118), channel_id=1, source_target_pairs={{0,256},{16,272},{32,288},{48,304},{64,320},{80,336},{96,352},{112... | collective-permute-start | bytes 638984 | tf_op jit(solution)/shard_map/ppermute | solution.py:20
  590.3 1.9 collective-permute-start.15
  592.3 1.7 fusion.74
  594.0 5.6 collective-permute-done.15
  599.6 4.5 collective-permute-start.12
  604.4 4.4 collective-permute-done.12
  608.8 0.8 add_add_fusion
  609.7 1.5 conditional.7
  609.7 1.5 fusion.3
  611.2 1.2 copy-done.5
  (44 shorter events, 1.4 us)
Async XLA Ops:
  6.5 222.6 %copy-start = (bf16[1,1664,512]{2,1,0:T(8,128)(2,1)S(1)}, bf16[1,1664,512]{2,1,0:T(8,128)(2,1)}, u32[]{:S(2)}) copy-start(bf16[1,1664,512]{2,1,0:T(8,128)(2,1)} %param.15) | copy-start | bytes 5111812
  6.5 507.1 %all-reduce.3.cloned.1.call-start = ((), (), s32[]{:S(2)}) async-start(), calls=%async_computation | async-start | bytes 2129920 | tf_op jit(solution)/shard_map/psum | solution.py:75
  228.5 3.4 copy-start.10
  228.5 3.4 copy-start.8
  229.2 4.0 copy-start.3
  235.3 0.7 copy-start.6
  235.4 0.7 copy-start.7
  513.7 40.8 %copy-start.11 = (bf16[64,1664]{1,0:T(8,128)(2,1)S(1)}, bf16[64,1664]{1,0:T(8,128)(2,1)}, u32[]{:S(2)}) copy-start(bf16[64,1664]{1,0:T(8,128)(2,1)} %get-tuple-element.104) | copy-start | bytes 638980
  514.8 30.3 %collective-permute-start = (bf16[64,1664]{1,0:T(8,128)(2,1)S(1)}, bf16[64,1664]{1,0:T(8,128)(2,1)S(1)}, u32[]{:S(2)}, u32[]{:S(2)}) collective-permute-start(bf16[64,1664]{1,0:T(8,128)(2,1)S(1)} %get-tuple-element.129), channel_id=1, source_target_pairs={{256,0},{272,16},{288,32},{304,48},{320,64},{336,80},{352,96},{368... | collective-permute-start | bytes 638984 | tf_op jit(solution)/shard_map/ppermute | solution.py:20
  516.1 36.5 %collective-permute-start.1 = (bf16[64,1664]{1,0:T(8,128)(2,1)S(1)}, bf16[64,1664]{1,0:T(8,128)(2,1)S(1)}, u32[]{:S(2)}, u32[]{:S(2)}) collective-permute-start(bf16[64,1664]{1,0:T(8,128)(2,1)S(1)} %get-tuple-element.129), channel_id=1, source_target_pairs={{0,256},{16,272},{32,288},{48,304},{64,320},{80,336},{96,352},{112... | collective-permute-start | bytes 638984 | tf_op jit(solution)/shard_map/ppermute | solution.py:20
  522.2 12.4 %collective-permute-start.5 = (bf16[64,1664]{1,0:T(8,128)(2,1)S(1)}, bf16[64,1664]{1,0:T(8,128)(2,1)S(1)}, u32[]{:S(2)}, u32[]{:S(2)}) collective-permute-start(bf16[64,1664]{1,0:T(8,128)(2,1)S(1)} %get-tuple-element.128), channel_id=1, source_target_pairs={{0,256},{256,0},{16,272},{272,16},{32,288},{288,32},{48,304},{304,... | collective-permute-start | bytes 638984 | tf_op jit(solution)/shard_map/ppermute | solution.py:14
  525.9 58.1 %collective-permute-start.3 = (bf16[64,1664]{1,0:T(8,128)(2,1)}, bf16[64,1664]{1,0:T(8,128)(2,1)}, u32[]{:S(2)}, u32[]{:S(2)}) collective-permute-start(bf16[64,1664]{1,0:T(8,128)(2,1)} %get-tuple-element.124), channel_id=1, source_target_pairs={{256,0},{272,16},{288,32},{304,48},{320,64},{336,80},{352,96},{368... | collective-permute-start | bytes 638984 | tf_op jit(solution)/shard_map/ppermute | solution.py:20
  527.1 63.2 %collective-permute-start.4 = (bf16[64,1664]{1,0:T(8,128)(2,1)}, bf16[64,1664]{1,0:T(8,128)(2,1)}, u32[]{:S(2)}, u32[]{:S(2)}) collective-permute-start(bf16[64,1664]{1,0:T(8,128)(2,1)} %get-tuple-element.124), channel_id=1, source_target_pairs={{0,256},{16,272},{32,288},{48,304},{64,320},{80,336},{96,352},{112... | collective-permute-start | bytes 638984 | tf_op jit(solution)/shard_map/ppermute | solution.py:20
  534.6 9.3 %collective-permute-start.2 = (bf16[64,1664]{1,0:T(8,128)(2,1)S(1)}, bf16[64,1664]{1,0:T(8,128)(2,1)S(1)}, u32[]{:S(2)}, u32[]{:S(2)}) collective-permute-start(bf16[64,1664]{1,0:T(8,128)(2,1)S(1)} %get-tuple-element.125), channel_id=1, source_target_pairs={{0,256},{256,0},{16,272},{272,16},{32,288},{288,32},{48,304},{304,... | collective-permute-start | bytes 638984 | tf_op jit(solution)/shard_map/ppermute | solution.py:14
  543.8 30.9 %collective-permute-start.7 = (bf16[64,1664]{1,0:T(8,128)(2,1)}, bf16[64,1664]{1,0:T(8,128)(2,1)}, u32[]{:S(2)}, u32[]{:S(2)}) collective-permute-start(bf16[64,1664]{1,0:T(8,128)(2,1)} %get-tuple-element.127), channel_id=1, source_target_pairs={{256,0},{272,16},{288,32},{304,48},{320,64},{336,80},{352,96},{368... | collective-permute-start | bytes 638984 | tf_op jit(solution)/shard_map/ppermute | solution.py:20
  545.1 35.6 %collective-permute-start.8 = (bf16[64,1664]{1,0:T(8,128)(2,1)}, bf16[64,1664]{1,0:T(8,128)(2,1)}, u32[]{:S(2)}, u32[]{:S(2)}) collective-permute-start(bf16[64,1664]{1,0:T(8,128)(2,1)} %get-tuple-element.127), channel_id=1, source_target_pairs={{0,256},{16,272},{32,288},{48,304},{64,320},{80,336},{96,352},{112... | collective-permute-start | bytes 638984 | tf_op jit(solution)/shard_map/ppermute | solution.py:20
  552.6 9.8 %collective-permute-start.6 = (bf16[64,1664]{1,0:T(8,128)(2,1)}, bf16[64,1664]{1,0:T(8,128)(2,1)}, u32[]{:S(2)}, u32[]{:S(2)}) collective-permute-start(bf16[64,1664]{1,0:T(8,128)(2,1)} %get-tuple-element.126), channel_id=1, source_target_pairs={{0,256},{256,0},{16,272},{272,16},{32,288},{288,32},{48,304},{304,... | collective-permute-start | bytes 638984 | tf_op jit(solution)/shard_map/ppermute | solution.py:14
  556.1 27.9 %copy-start.1 = (f32[1664,512]{1,0:T(8,128)}, f32[1664,512]{1,0:T(8,128)S(1)}, u32[]{:S(2)}) copy-start(f32[1664,512]{1,0:T(8,128)S(1)} %get-tuple-element.138) | copy-start | bytes 10223620
  562.4 11.0 %collective-permute-start.9 = (bf16[64,1664]{1,0:T(8,128)(2,1)}, bf16[64,1664]{1,0:T(8,128)(2,1)S(1)}, u32[]{:S(2)}, u32[]{:S(2)}) collective-permute-start(bf16[64,1664]{1,0:T(8,128)(2,1)} %get-tuple-element.121), channel_id=1, source_target_pairs={{0,256},{256,0},{16,272},{272,16},{32,288},{288,32},{48,304},{304,... | collective-permute-start | bytes 638984 | tf_op jit(solution)/shard_map/ppermute | solution.py:14
  573.4 31.0 %collective-permute-start.10 = (bf16[64,1664]{1,0:T(8,128)(2,1)}, bf16[64,1664]{1,0:T(8,128)(2,1)S(1)}, u32[]{:S(2)}, u32[]{:S(2)}) collective-permute-start(bf16[64,1664]{1,0:T(8,128)(2,1)} %get-tuple-element.120), channel_id=1, source_target_pairs={{256,0},{272,16},{288,32},{304,48},{320,64},{336,80},{352,96},{368... | collective-permute-start | bytes 638984 | tf_op jit(solution)/shard_map/ppermute | solution.py:20
  574.7 29.7 %collective-permute-start.11 = (bf16[64,1664]{1,0:T(8,128)(2,1)}, bf16[64,1664]{1,0:T(8,128)(2,1)S(1)}, u32[]{:S(2)}, u32[]{:S(2)}) collective-permute-start(bf16[64,1664]{1,0:T(8,128)(2,1)} %get-tuple-element.120), channel_id=1, source_target_pairs={{0,256},{16,272},{32,288},{48,304},{64,320},{80,336},{96,352},{112... | collective-permute-start | bytes 638984 | tf_op jit(solution)/shard_map/ppermute | solution.py:20
  580.8 11.5 %copy-start.4 = (bf16[4,64,512]{2,1,0:T(8,128)(2,1)S(1)}, bf16[4,64,512]{2,1,0:T(8,128)(2,1)}, u32[]{:S(2)}) copy-start(bf16[4,64,512]{2,1,0:T(8,128)(2,1)} %copy-done.3) | copy-start | bytes 786436
  580.8 11.5 %copy-start.9 = (bf16[1,64,512]{2,0,1:T(2,128)(2,1)S(1)}, bf16[1,64,512]{2,0,1:T(2,128)(2,1)}, u32[]{:S(2)}) copy-start(bf16[1,64,512]{2,0,1:T(2,128)(2,1)} %copy-done.8) | copy-start | bytes 196612
  580.8 23.3 %collective-permute-start.13 = (bf16[64,1664]{1,0:T(8,128)(2,1)S(1)}, bf16[64,1664]{1,0:T(8,128)(2,1)S(1)}, u32[]{:S(2)}, u32[]{:S(2)}) collective-permute-start(bf16[64,1664]{1,0:T(8,128)(2,1)S(1)} %get-tuple-element.118), channel_id=1, source_target_pairs={{256,0},{272,16},{288,32},{304,48},{320,64},{336,80},{352,96},{368... | collective-permute-start | bytes 638984 | tf_op jit(solution)/shard_map/ppermute | solution.py:20
  584.0 24.8 %copy-start.2 = (f32[1664,512]{1,0:T(8,128)S(1)}, f32[1664,512]{1,0:T(8,128)}, u32[]{:S(2)}) copy-start(f32[1664,512]{1,0:T(8,128)} %copy-done.1) | copy-start | bytes 10223620
  584.0 20.1 %collective-permute-start.14 = (bf16[64,1664]{1,0:T(8,128)(2,1)S(1)}, bf16[64,1664]{1,0:T(8,128)(2,1)S(1)}, u32[]{:S(2)}, u32[]{:S(2)}) collective-permute-start(bf16[64,1664]{1,0:T(8,128)(2,1)S(1)} %get-tuple-element.118), channel_id=1, source_target_pairs={{0,256},{16,272},{32,288},{48,304},{64,320},{80,336},{96,352},{112... | collective-permute-start | bytes 638984 | tf_op jit(solution)/shard_map/ppermute | solution.py:20
  590.3 9.2 %collective-permute-start.15 = (bf16[64,1664]{1,0:T(8,128)(2,1)S(1)}, bf16[64,1664]{1,0:T(8,128)(2,1)S(1)}, u32[]{:S(2)}, u32[]{:S(2)}) collective-permute-start(bf16[64,1664]{1,0:T(8,128)(2,1)S(1)} %fusion.41), channel_id=1, source_target_pairs={{0,256},{256,0},{16,272},{272,16},{32,288},{288,32},{48,304},{304,... | collective-permute-start | bytes 638984 | tf_op jit(solution)/shard_map/ppermute | solution.py:14
  599.6 9.2 %collective-permute-start.12 = (bf16[64,1664]{1,0:T(8,128)(2,1)S(1)}, bf16[64,1664]{1,0:T(8,128)(2,1)S(1)}, u32[]{:S(2)}, u32[]{:S(2)}) collective-permute-start(bf16[64,1664]{1,0:T(8,128)(2,1)S(1)} %get-tuple-element.119), channel_id=1, source_target_pairs={{0,256},{256,0},{16,272},{272,16},{32,288},{288,32},{48,304},{304,... | collective-permute-start | bytes 638984 | tf_op jit(solution)/shard_map/ppermute | solution.py:14
  611.1 1.2 copy-start.5
Sparse Core Ops, SparseCore 0:
  236.3 277.3 all-reduce.2
where the time goes:
time: 620 us; the launch traced here: 619 us
  waiting for transfers between devices  307 us (50%)
  blocking collectives  219 us (35%)
  starting transfers between devices  54 us (9%)
  between operations  13.8 us (2%)
  matrix products  11.2 us (2%)
  other arithmetic  9.54 us (2%)
    psum x1, waiting for transfers between devices, local(): lax.psum(product.astype(jnp.bfloat16), 'tensor').astype(jnp.float32)  278 us
    all_gather x1, blocking collectives, local(): lax.all_gather(inputs, 'section', axis=1, tiled=True)  115 us
    all_gather x1, blocking collectives, local(): lax.all_gather(cotangent, 'section', axis=1, tiled=True)  104 us
    ppermute x10, starting transfers between devices, from_behind(): lax.ppermute(value, axis, [(source, source + steps) for source in range(i...  39.9 us
    ppermute x6, waiting for transfers between devices, swapped(): return lax.ppermute(block, axis, route)  29.7 us
    ppermute x6, starting transfers between devices, swapped(): return lax.ppermute(block, axis, route)  14.1 us
  transfers between devices with their start and end apart: 17, of which 6 were waited for; matrix products, arithmetic and copies ran while one was open for 2% of the time, Pallas kernels for 0%

commit v1 on v0

v1 whole, which is shorter than its diff:
```python
import jax
import jax.numpy as jnp
import numpy as np
from jax import lax
from jax.sharding import Mesh, PartitionSpec as P

SECTION = ("half", "yl", "zl")
TENSOR = ("zh", "x", "core")
OWNERS = ("half", "x", "core")


def local(inputs, cotangent, plan, weights):
    piece = weights[0]
    width = piece.shape[1]
    hidden_units = piece.shape[0]
    sections = lax.axis_size(SECTION)
    owners = lax.axis_size(OWNERS)

    entering = jnp.take(inputs, plan, axis=0).reshape(1, -1, width)
    returning = cotangent.reshape(1, -1, width)
    outgoing = jnp.concatenate(
        [
            jnp.broadcast_to(entering, (sections // 2,) + entering.shape[1:]),
            jnp.broadcast_to(returning, (sections // 2,) + returning.shape[1:]),
        ]
    )
    rows = lax.all_to_all(outgoing, SECTION, 0, 0).reshape(-1, width)
    row_count = rows.shape[0]

    partial = jnp.einsum("rd,fd->rf", rows, piece, preferred_element_type=jnp.float32)
    partial = partial.astype(jnp.bfloat16).reshape(owners, row_count // owners, hidden_units)
    gathered = lax.all_to_all(partial, OWNERS, 0, 0)
    gathered = gathered.reshape((2, owners // 2) + gathered.shape[1:])
    near = jnp.sum(gathered.astype(jnp.float32), axis=1).astype(jnp.bfloat16)
    far = lax.ppermute(near, "zh", [(0, 1), (1, 0)])
    total = near.astype(jnp.float32) + far.astype(jnp.float32)
    pre_sum = total[0]
    grad_hidden = total[1].astype(jnp.bfloat16).astype(jnp.float32)
    logistic = jax.nn.sigmoid(pre_sum)
    hidden = (pre_sum * logistic).astype(jnp.bfloat16)
    grad_pre = (grad_hidden * logistic * (1.0 + pre_sum * (1.0 - logistic))).astype(jnp.bfloat16)

    answer = jnp.concatenate(
        [
            jnp.broadcast_to(grad_pre[None], (owners // 2,) + grad_pre.shape),
            jnp.broadcast_to(hidden[None], (owners // 2,) + hidden.shape),
        ]
    )
    left = lax.all_to_all(answer, OWNERS, 0, 0).reshape(row_count, hidden_units)
    grads = jnp.einsum("rf,rd->fd", left, rows, preferred_element_type=jnp.float32)
    return grads.astype(jnp.bfloat16)[None]


def solution(mesh):
    fine = Mesh(
        np.asarray(mesh.devices).reshape(2, 2, 8, 2, 4, 2),
        ("half", "yl", "zl", "zh", "x", "core"),
    )
    placed = (
        P(None, SECTION, TENSOR),
        P(None, SECTION, TENSOR),
        P(),
        P(SECTION, None, TENSOR),
    )
    return jax.shard_map(
        local, mesh=fine, in_specs=placed, out_specs=P(SECTION, None, TENSOR), check_vma=False
    )
```

time: 620 us -> 101 us (0.16)
  the two profiles are of different devices: /device:TPU:8 before, /device:TPU:1 now
where the time goes in v1:
time: 101 us
  blocking collectives  74.6 us (74%)
  waiting for transfers between devices  11.5 us (11%)
  starting transfers between devices  7.93 us (8%)
  matrix products  2.52 us (2%)
  local copies, waits for them, and re-layouts  2.25 us (2%)
  other arithmetic  1.83 us (2%)
    all_to_all x1, blocking collectives, local(): rows = lax.all_to_all(outgoing, SECTION, 0, 0).reshape(-1, width)  34.6 us
    all_to_all x1, blocking collectives, local(): gathered = lax.all_to_all(partial, OWNERS, 0, 0)  20.8 us
    all_to_all x1, blocking collectives, local(): left = lax.all_to_all(answer, OWNERS, 0, 0).reshape(row_count, hidden_units)  19.2 us
    ppermute x1, waiting for transfers between devices, local(): far = lax.ppermute(near, 'zh', [(0, 1), (1, 0)])  11.5 us
    ppermute x1, starting transfers between devices, local(): far = lax.ppermute(near, 'zh', [(0, 1), (1, 0)])  7.93 us
  transfers between devices with their start and end apart: 1, of which 1 were waited for; matrix products, arithmetic and copies ran while one was open for 0% of the time, Pallas kernels for 0%

profile of v1, /device:TPU:1, one launch (start us, length us, event | category | flops | bytes accessed | tf_op | source)
XLA Modules:
  0.0 100.7 jit_solution(5670758910279511808)
XLA Ops:
  0.0 0.0 copy-start
  0.0 0.8 compare_and_fusion
  0.8 0.7 compare_select_fusion
  1.4 0.1 broadcast_in_dim.47
  1.5 0.1 broadcast_in_dim.48
  1.6 1.3 %gather_fusion = bf16[4,2,512]{2,1,0:T(2,128)(2,1)S(1)} fusion(bf16[4,2,512]{2,1,0:T(2,128)(2,1)} %param.4, s32[1024]{0:T(1024)S(1)} %pad_clamp_fusion), kind=kCustom, calls=%fused_computation | custom fusion | bytes 16400 | tf_op jit(solution)/shard_map/jit(_take)/gather | solution.py:19
  2.9 0.7 broadcast_in_dim.53
  3.6 0.1 broadcast_select_fusion
  3.8 34.6 %all_to_all.15 = bf16[32,8,512]{2,1,0:T(8,128)(2,1)S(1)} all-to-all(bf16[32,8,512]{2,1,0:T(8,128)(2,1)S(1)} %pad_maximum_fusion.1), channel_id=1, replica_groups=mesh['half'=2,'yl'=2,'zl'=8,'zh'=2,'x'=4,'core'=2] {'half','yl','zl'}, dimensions={0} | all-to-all | bytes 524288 | tf_op jit(solution)/shard_map/all_to_all | solution.py:27
  38.4 0.0 copy-done
  38.4 0.7 convolution_convert_fusion.1
  39.1 20.8 %all_to_all.16 = bf16[16,16,1664]{2,1,0:T(8,128)(2,1)S(1)} all-to-all(bf16[16,16,1664]{2,1,0:T(8,128)(2,1)S(1)} %bitcast.20), channel_id=1, replica_groups=mesh['half'=2,'yl'=2,'zl'=8,'zh'=2,'x'=4,'core'=2] {'half','x','core'}, dimensions={0} | all-to-all | bytes 1703936 | tf_op jit(solution)/shard_map/all_to_all | solution.py:32
  59.9 0.1 bitcast_reduce_fusion
  60.0 7.9 %collective-permute-start = (bf16[2,16,1664]{2,1,0:T(8,128)(2,1)S(1)}, bf16[2,16,1664]{2,1,0:T(8,128)(2,1)S(1)}, u32[]{:S(2)}, u32[]{:S(2)}) collective-permute-start(bf16[2,16,1664]{2,1,0:T(8,128)(2,1)S(1)} %bitcast_reduce_fusion), channel_id=1, source_target_pairs={{0,8},{8,0},{1,9},{9,1},{2,10},{10,2},{3,11},{11,3},{4,12},{12,4},... | collective-permute-start | bytes 319496 | tf_op jit(solution)/shard_map/ppermute | solution.py:35
  68.0 11.5 %collective-permute-done = bf16[2,16,1664]{2,1,0:T(8,128)(2,1)S(1)} collective-permute-done((bf16[2,16,1664]{2,1,0:T(8,128)(2,1)S(1)}, bf16[2,16,1664]{2,1,0:T(8,128)(2,1)S(1)}, u32[]{:S(2)}, u32[]{:S(2)}) %collective-permute-start) | collective-permute-done | bytes 106528 | tf_op jit(solution)/shard_map/ppermute | solution.py:35
  79.5 0.1 fusion.5
  79.6 0.1 pad_maximum_fusion
  79.7 19.2 %all_to_all.17 = bf16[16,16,1664]{2,1,0:T(8,128)(2,1)S(1)} all-to-all(bf16[16,16,1664]{2,1,0:T(8,128)(2,1)S(1)} %pad_maximum_fusion), channel_id=1, replica_groups=mesh['half'=2,'yl'=2,'zl'=8,'zh'=2,'x'=4,'core'=2] {'half','x','core'}, dimensions={0} | all-to-all | bytes 1703936 | tf_op jit(solution)/shard_map/all_to_all | solution.py:49
  98.9 1.8 %fusion = bf16[1,1664,512]{2,1,0:T(8,128)(2,1)} fusion(bf16[256,1664]{1,0:T(8,128)(2,1)S(1)} %bitcast.19, bf16[32,8,512]{2,1,0:T(8,128)(2,1)S(1)} %all_to_all.15), kind=kOutput, calls=%fused_computation.2 | convolution fusion | flops 437059584 | bytes 2818048 | tf_op jit(solution)/shard_map/rf,rd->fd/dot_general | solution.py:50
  (8 shorter events, 0.2 us)
Async XLA Ops:
  0.0 38.4 %copy-start = (bf16[1,1664,512]{2,1,0:T(8,128)(2,1)S(1)}, bf16[1,1664,512]{2,1,0:T(8,128)(2,1)}, u32[]{:S(2)}) copy-start(bf16[1,1664,512]{2,1,0:T(8,128)(2,1)} %param.7) | copy-start | bytes 5111812
  60.0 19.4 %collective-permute-start = (bf16[2,16,1664]{2,1,0:T(8,128)(2,1)S(1)}, bf16[2,16,1664]{2,1,0:T(8,128)(2,1)S(1)}, u32[]{:S(2)}, u32[]{:S(2)}) collective-permute-start(bf16[2,16,1664]{2,1,0:T(8,128)(2,1)S(1)} %bitcast_reduce_fusion), channel_id=1, source_target_pairs={{0,8},{8,0},{1,9},{9,1},{2,10},{10,2},{3,11},{11,3},{4,12},{12,4},... | collective-permute-start | bytes 319496 | tf_op jit(solution)/shard_map/ppermute | solution.py:35

commit v2 on v1

v2 whole, which is shorter than its diff:
```python
import jax
import jax.numpy as jnp
import numpy as np
from jax import lax
from jax.experimental import pallas as pl
from jax.experimental.pallas import tpu as pltpu
from jax.sharding import Mesh, PartitionSpec as P

SECTION = ("half", "yl", "zl")
TENSOR = ("zh", "x", "core")
OWNERS = ("half", "x")


def pack_kernel(plan_ref, inputs_ref, cotangent_ref, out_ref):
    batches = inputs_ref.shape[0]
    half = out_ref.shape[0] // 2
    entering = jnp.concatenate(
        [inputs_ref[plan_ref[k]].astype(jnp.float32) for k in range(batches)], axis=0
    )
    returning = jnp.concatenate(
        [cotangent_ref[k].astype(jnp.float32) for k in range(batches)], axis=0
    )
    for first, rows in ((0, entering), (half, returning)):
        rows = rows.astype(out_ref.dtype)
        out_ref[pl.ds(first, half)] = jnp.broadcast_to(rows[None], (half,) + rows.shape)


def pack(plan, inputs, cotangent, sections):
    batches, tokens, width = inputs.shape
    return pl.pallas_call(
        pack_kernel,
        out_shape=jax.ShapeDtypeStruct((sections, batches * tokens, width), inputs.dtype),
        in_specs=[
            pl.BlockSpec(memory_space=pltpu.SMEM),
            pl.BlockSpec(memory_space=pltpu.VMEM),
            pl.BlockSpec(memory_space=pltpu.VMEM),
        ],
        out_specs=pl.BlockSpec(memory_space=pltpu.VMEM),
    )(plan, inputs, cotangent)


def local(inputs, cotangent, plan, weights):
    piece = weights[0]
    hidden_units, width = piece.shape
    sections = lax.axis_size(SECTION)
    owners = lax.axis_size(OWNERS)
    core = lax.axis_index("core")
    twin = [(0, 1), (1, 0)]

    rows = lax.all_to_all(pack(plan, inputs, cotangent, sections), SECTION, 0, 0)
    rows = rows.reshape(2, -1, width)
    half_rows = rows.shape[1]
    rows_here = lax.dynamic_index_in_dim(rows, core, 0, keepdims=False)
    rows_there = lax.dynamic_index_in_dim(rows, 1 - core, 0, keepdims=False)

    def project(values):
        return jnp.einsum("rd,fd->rf", values, piece, preferred_element_type=jnp.float32).astype(
            jnp.bfloat16
        )

    arrived = lax.ppermute(project(rows_there), "core", twin)
    partial = project(rows_here).astype(jnp.float32) + arrived.astype(jnp.float32)
    partial = partial.astype(jnp.bfloat16).reshape(owners, half_rows // owners, hidden_units)
    gathered = lax.all_to_all(partial, OWNERS, 0, 0)
    gathered = gathered.reshape((2, owners // 2) + gathered.shape[1:])
    near = jnp.sum(gathered.astype(jnp.float32), axis=1).astype(jnp.bfloat16)
    far = lax.ppermute(near, "zh", twin)
    total = near.astype(jnp.float32) + far.astype(jnp.float32)
    pre_sum = total[0]
    grad_hidden = total[1].astype(jnp.bfloat16).astype(jnp.float32)
    logistic = jax.nn.sigmoid(pre_sum)
    hidden = (pre_sum * logistic).astype(jnp.bfloat16)
    grad_pre = (grad_hidden * logistic * (1.0 + pre_sum * (1.0 - logistic))).astype(jnp.bfloat16)

    answer = jnp.concatenate(
        [
            jnp.broadcast_to(grad_pre[None], (owners // 2,) + grad_pre.shape),
            jnp.broadcast_to(hidden[None], (owners // 2,) + hidden.shape),
        ]
    )
    left_here = lax.all_to_all(answer, OWNERS, 0, 0).reshape(half_rows, hidden_units)
    left_there = lax.ppermute(left_here, "core", twin)
    grads = jnp.einsum(
        "rf,rd->fd",
        jnp.concatenate([left_here, left_there]),
        jnp.concatenate([rows_here, rows_there]),
        preferred_element_type=jnp.float32,
    )
    return grads.astype(jnp.bfloat16)[None]


def solution(mesh):
    fine = Mesh(
        np.asarray(mesh.devices).reshape(2, 2, 8, 2, 4, 2),
        ("half", "yl", "zl", "zh", "x", "core"),
    )
    placed = (
        P(None, SECTION, TENSOR),
        P(None, SECTION, TENSOR),
        P(),
        P(SECTION, None, TENSOR),
    )
    return jax.shard_map(
        local, mesh=fine, in_specs=placed, out_specs=P(SECTION, None, TENSOR), check_vma=False
    )
```

time: 101 us -> 96.2 us (0.952)
  blocking collectives: 74.6 us -> 25.4 us
  starting transfers between devices: 7.93 us -> 32.3 us
  waiting for transfers between devices: 11.5 us -> 33 us
  local copies, waits for them, and re-layouts: 2.25 us -> 0.06 us
  other arithmetic: 1.83 us -> 0.18 us
  Pallas kernels: 0 us -> 1.58 us
    all_to_all x2 -> x1, blocking collectives: 53.8 us -> 11.2 us  [local(): lax.all_to_all(answer, OWNERS, 0, 0).reshape(half_rows, hidden_units)]
    all_to_all x0 -> x1, waiting for transfers between devices: none -> 18.7 us  [local(): lax.all_to_all(pack(plan, inputs, cotangent, sections), SECTION, 0, 0)]
    all_to_all x0 -> x1, starting transfers between devices: none -> 16.1 us  [local(): lax.all_to_all(pack(plan, inputs, cotangent, sections), SECTION, 0, 0)]
    ppermute x1 -> x3, starting transfers between devices: 7.93 us -> 16.2 us  [the longest x1 7.94 us: local(): far = lax.ppermute(near, 'zh', twin)]
    all_to_all x1, blocking collectives: 20.8 us -> 14.2 us  [local(): gathered = lax.all_to_all(partial, OWNERS, 0, 0)]
    ppermute x1 -> x3, waiting for transfers between devices: 11.5 us -> 14.2 us  [the longest x1 11.5 us: local(): far = lax.ppermute(near, 'zh', twin)]
    pallas_call x0 -> x1, Pallas kernels: none -> 1.58 us  [pack(): pl.pallas_call(pack_kernel, out_shape=jax.ShapeDtypeStruct((sections, bat...]
    gather x2 -> x0, local copies, waits for them, and re-layouts: 1.29 us -> none  [local(): entering = jnp.take(inputs, plan, axis=0).reshape(1, -1, width)]
  transfers between devices with their start and end apart: 1 -> 4, of which waited for: 1 -> 4; matrix products, arithmetic and copies ran while one was open for 0% -> 0% of each run, Pallas kernels for 0% -> 0%
where the time goes in v2:
time: 96.2 us; the launch traced here: 95.8 us
  waiting for transfers between devices  33 us (34%)
  starting transfers between devices  32.3 us (34%)
  blocking collectives  25.4 us (26%)
  matrix products  3.18 us (3%)
  Pallas kernels  1.58 us (2%)
    all_to_all x1, waiting for transfers between devices, local(): lax.all_to_all(pack(plan, inputs, cotangent, sections), SECTION, 0, 0)  18.7 us
    all_to_all x1, starting transfers between devices, local(): lax.all_to_all(pack(plan, inputs, cotangent, sections), SECTION, 0, 0)  16.1 us
    all_to_all x1, blocking collectives, local(): gathered = lax.all_to_all(partial, OWNERS, 0, 0)  14.2 us
    ppermute x1, waiting for transfers between devices, local(): far = lax.ppermute(near, 'zh', twin)  11.5 us
    all_to_all x1, blocking collectives, local(): lax.all_to_all(answer, OWNERS, 0, 0).reshape(half_rows, hidden_units)  11.2 us
    ppermute x1, starting transfers between devices, local(): far = lax.ppermute(near, 'zh', twin)  7.94 us
    ppermute x1, starting transfers between devices, local(): left_there = lax.ppermute(left_here, 'core', twin)  4.59 us
    ppermute x1, starting transfers between devices, local(): arrived = lax.ppermute(project(rows_there), 'core', twin)  3.66 us
  transfers between devices with their start and end apart: 4, of which 4 were waited for; matrix products, arithmetic and copies ran while one was open for 0% of the time, Pallas kernels for 0%

profile of v2, /device:TPU:1, one launch (start us, length us, event | category | flops | bytes accessed | tf_op | source)
XLA Modules:
  0.0 95.8 jit_solution(12648142050940730837)
XLA Ops:
  0.0 0.0 copy-start
  0.0 1.6 %shard_map.46 = bf16[32,8,512]{2,1,0:T(8,128)(2,1)} custom-call(s32[4]{0:T(128)} %plan_ref.1, bf16[4,2,512]{2,1,0:T(2,128)(2,1)} %inputs_ref.1, bf16[4,2,512]{2,1,0:T(2,128)(2,1)} %cotangent_ref.1), custom_call_target="tpu_custom_call" | custom-call | tf_op jit(solution)/shard_map/pallas_call | solution.py:30
  1.6 16.1 %all-to-all-start = ((bf16[32,8,512]{2,1,0:T(8,128)(2,1)}), bf16[32,8,512]{2,1,0:T(8,128)(2,1)S(1)}, u32[]{:S(2)}, u32[]{:S(2)}) async-start(bf16[32,8,512]{2,1,0:T(8,128)(2,1)} %shard_map.46), calls=%async_computation | async-start | bytes 524288 | tf_op jit(solution)/shard_map/all_to_all | solution.py:50
  17.7 18.7 %all-to-all-done = bf16[32,8,512]{2,1,0:T(8,128)(2,1)S(1)} async-done(((bf16[32,8,512]{2,1,0:T(8,128)(2,1)}), bf16[32,8,512]{2,1,0:T(8,128)(2,1)S(1)}, u32[]{:S(2)}, u32[]{:S(2)}) %all-to-all-start) | async-done | bytes 262176 | tf_op jit(solution)/shard_map/all_to_all | solution.py:50
  36.5 0.0 copy-done
  36.5 0.7 convolution_convert_fusion.1
  37.1 3.7 %collective-permute-start = (bf16[128,1664]{1,0:T(8,128)(2,1)S(1)}, bf16[128,1664]{1,0:T(8,128)(2,1)S(1)}, u32[]{:S(2)}, u32[]{:S(2)}) collective-permute-start(bf16[128,1664]{1,0:T(8,128)(2,1)S(1)} %convolution_convert_fusion.1), channel_id=1, source_target_pairs={{0,1},{1,0},{2,3},{3,2},{4,5},{5,4},{6,7},{7,6},{8,9},{9,8},{10,11... | collective-permute-start | bytes 1277960 | tf_op jit(solution)/shard_map/ppermute | solution.py:61
  40.8 1.4 %collective-permute-done = bf16[128,1664]{1,0:T(8,128)(2,1)S(1)} collective-permute-done((bf16[128,1664]{1,0:T(8,128)(2,1)S(1)}, bf16[128,1664]{1,0:T(8,128)(2,1)S(1)}, u32[]{:S(2)}, u32[]{:S(2)}) %collective-permute-start) | collective-permute-done | bytes 426016 | tf_op jit(solution)/shard_map/ppermute | solution.py:61
  42.2 0.7 add_convert_fusion
  42.9 14.2 %all_to_all.15 = bf16[8,16,1664]{2,1,0:T(8,128)(2,1)S(1)} all-to-all(bf16[8,16,1664]{2,1,0:T(8,128)(2,1)S(1)} %bitcast.24), channel_id=1, replica_groups=mesh['half'=2,'yl'=2,'zl'=8,'zh'=2,'x'=4,'core'=2] {'half','x'}, dimensions={0} | all-to-all | bytes 851968 | tf_op jit(solution)/shard_map/all_to_all | solution.py:64
  57.1 0.1 bitcast_reduce_fusion
  57.2 7.9 %collective-permute-start.1 = (bf16[2,16,1664]{2,1,0:T(8,128)(2,1)S(1)}, bf16[2,16,1664]{2,1,0:T(8,128)(2,1)S(1)}, u32[]{:S(2)}, u32[]{:S(2)}) collective-permute-start(bf16[2,16,1664]{2,1,0:T(8,128)(2,1)S(1)} %bitcast_reduce_fusion), channel_id=1, source_target_pairs={{0,8},{8,0},{1,9},{9,1},{2,10},{10,2},{3,11},{11,3},{4,12},{12,4},... | collective-permute-start | bytes 319496 | tf_op jit(solution)/shard_map/ppermute | solution.py:67
  65.1 11.5 %collective-permute-done.1 = bf16[2,16,1664]{2,1,0:T(8,128)(2,1)S(1)} collective-permute-done((bf16[2,16,1664]{2,1,0:T(8,128)(2,1)S(1)}, bf16[2,16,1664]{2,1,0:T(8,128)(2,1)S(1)}, u32[]{:S(2)}, u32[]{:S(2)}) %collective-permute-start.1) | collective-permute-done | bytes 106528 | tf_op jit(solution)/shard_map/ppermute | solution.py:67
  76.6 0.1 fusion.11
  76.8 11.2 %all_to_all.16 = bf16[8,16,1664]{2,1,0:T(8,128)(2,1)S(1)} all-to-all(bf16[8,16,1664]{2,1,0:T(8,128)(2,1)S(1)} %pad_maximum_fusion), channel_id=1, replica_groups=mesh['half'=2,'yl'=2,'zl'=8,'zh'=2,'x'=4,'core'=2] {'half','x'}, dimensions={0} | all-to-all | bytes 851968 | tf_op jit(solution)/shard_map/all_to_all | solution.py:81
  88.0 4.6 %collective-permute-start.2 = (bf16[128,1664]{1,0:T(8,128)(2,1)S(1)}, bf16[128,1664]{1,0:T(8,128)(2,1)S(1)}, u32[]{:S(2)}, u32[]{:S(2)}) collective-permute-start(bf16[128,1664]{1,0:T(8,128)(2,1)S(1)} %bitcast.26), channel_id=1, source_target_pairs={{0,1},{1,0},{2,3},{3,2},{4,5},{5,4},{6,7},{7,6},{8,9},{9,8},{10,11... | collective-permute-start | bytes 1277960 | tf_op jit(solution)/shard_map/ppermute | solution.py:82
  92.6 1.4 %collective-permute-done.2 = bf16[128,1664]{1,0:T(8,128)(2,1)S(1)} collective-permute-done((bf16[128,1664]{1,0:T(8,128)(2,1)S(1)}, bf16[128,1664]{1,0:T(8,128)(2,1)S(1)}, u32[]{:S(2)}, u32[]{:S(2)}) %collective-permute-start.2) | collective-permute-done | bytes 426016 | tf_op jit(solution)/shard_map/ppermute | solution.py:82
  94.0 1.8 %fusion = bf16[1,1664,512]{2,1,0:T(8,128)(2,1)} fusion(bf16[128,1664]{1,0:T(8,128)(2,1)S(1)} %collective-permute-done.2, bf16[128,1664]{1,0:T(8,128)(2,1)S(1)} %bitcast.27, bf16[128,512]{1,0:T(8,128)(2,1)S(1)} %get-tuple-element.5, bf16[128,512]{1,0:T(8,128)(2,1)S(1)} %get-tuple-element.6), kind=kOutput, calls=%fused_computation.1 | convolution fusion | flops 439287808 | bytes 2818048 | tf_op jit(solution)/shard_map/rf,rd->fd/dot_general | solution.py:83
  (5 shorter events, 0.1 us)
Async XLA Ops:
  0.0 36.5 %copy-start = (bf16[1,1664,512]{2,1,0:T(8,128)(2,1)S(1)}, bf16[1,1664,512]{2,1,0:T(8,128)(2,1)}, u32[]{:S(2)}) copy-start(bf16[1,1664,512]{2,1,0:T(8,128)(2,1)} %param.7) | copy-start | bytes 5111812
  1.6 34.8 %all-to-all-start = ((bf16[32,8,512]{2,1,0:T(8,128)(2,1)}), bf16[32,8,512]{2,1,0:T(8,128)(2,1)S(1)}, u32[]{:S(2)}, u32[]{:S(2)}) async-start(bf16[32,8,512]{2,1,0:T(8,128)(2,1)} %shard_map.46), calls=%async_computation | async-start | bytes 524288 | tf_op jit(solution)/shard_map/all_to_all | solution.py:50
  37.1 5.0 %collective-permute-start = (bf16[128,1664]{1,0:T(8,128)(2,1)S(1)}, bf16[128,1664]{1,0:T(8,128)(2,1)S(1)}, u32[]{:S(2)}, u32[]{:S(2)}) collective-permute-start(bf16[128,1664]{1,0:T(8,128)(2,1)S(1)} %convolution_convert_fusion.1), channel_id=1, source_target_pairs={{0,1},{1,0},{2,3},{3,2},{4,5},{5,4},{6,7},{7,6},{8,9},{9,8},{10,11... | collective-permute-start | bytes 1277960 | tf_op jit(solution)/shard_map/ppermute | solution.py:61
  57.2 19.4 %collective-permute-start.1 = (bf16[2,16,1664]{2,1,0:T(8,128)(2,1)S(1)}, bf16[2,16,1664]{2,1,0:T(8,128)(2,1)S(1)}, u32[]{:S(2)}, u32[]{:S(2)}) collective-permute-start(bf16[2,16,1664]{2,1,0:T(8,128)(2,1)S(1)} %bitcast_reduce_fusion), channel_id=1, source_target_pairs={{0,8},{8,0},{1,9},{9,1},{2,10},{10,2},{3,11},{11,3},{4,12},{12,4},... | collective-permute-start | bytes 319496 | tf_op jit(solution)/shard_map/ppermute | solution.py:67
  88.0 6.0 %collective-permute-start.2 = (bf16[128,1664]{1,0:T(8,128)(2,1)S(1)}, bf16[128,1664]{1,0:T(8,128)(2,1)S(1)}, u32[]{:S(2)}, u32[]{:S(2)}) collective-permute-start(bf16[128,1664]{1,0:T(8,128)(2,1)S(1)} %bitcast.26), channel_id=1, source_target_pairs={{0,1},{1,0},{2,3},{3,2},{4,5},{5,4},{6,7},{7,6},{8,9},{9,8},{10,11... | collective-permute-start | bytes 1277960 | tf_op jit(solution)/shard_map/ppermute | solution.py:82

commit v3 on v2

--- a/solution.py
+++ b/solution.py
@@ -8,6 +8,7 @@
 
 SECTION = ("half", "yl", "zl")
 TENSOR = ("zh", "x", "core")
+ROOT = 4
 OWNERS = ("half", "x")
 
 
@@ -47,7 +48,8 @@
     core = lax.axis_index("core")
     twin = [(0, 1), (1, 0)]
 
-    rows = lax.all_to_all(pack(plan, inputs, cotangent, sections), SECTION, 0, 0)
+    order = [h * 16 + y * 8 + (z + ROOT) % 8 for h in range(2) for y in range(2) for z in range(8)]
+    rows = lax.all_to_all(pack(plan, inputs, cotangent, sections), SECTION, 0, 0, axis_index_groups=[order])
     rows = rows.reshape(2, -1, width)
     half_rows = rows.shape[1]
     rows_here = lax.dynamic_index_in_dim(rows, core, 0, keepdims=False)

time: 96.2 us -> 89.7 us (0.932)
  the two profiles are of different devices: /device:TPU:1 before, /device:TPU:33 now
where the time goes in v3:
time: 89.7 us; the launch traced here: 89.3 us
  starting transfers between devices  36.5 us (41%)
  blocking collectives  25.7 us (29%)
  waiting for transfers between devices  21.9 us (24%)
  matrix products  3.18 us (4%)
  Pallas kernels  1.58 us (2%)
    all_to_all x1, blocking collectives, local(): gathered = lax.all_to_all(partial, OWNERS, 0, 0)  14.8 us
    all_to_all x1, starting transfers between devices, local(): lax.all_to_all(pack(plan, inputs, cotangent, sections), SECTION, 0, 0, ax...  14 us
    all_to_all x1, blocking collectives, local(): lax.all_to_all(answer, OWNERS, 0, 0).reshape(half_rows, hidden_units)  10.9 us
    all_to_all x1, waiting for transfers between devices, local(): lax.all_to_all(pack(plan, inputs, cotangent, sections), SECTION, 0, 0, ax...  10.8 us
    ppermute x1, starting transfers between devices, local(): far = lax.ppermute(near, 'zh', twin)  9.57 us
    ppermute x1, waiting for transfers between devices, local(): far = lax.ppermute(near, 'zh', twin)  8.37 us
    ppermute x1, starting transfers between devices, local(): left_there = lax.ppermute(left_here, 'core', twin)  6.67 us
    ppermute x1, starting transfers between devices, local(): arrived = lax.ppermute(project(rows_there), 'core', twin)  6.34 us
  transfers between devices with their start and end apart: 4, of which 4 were waited for; matrix products, arithmetic and copies ran while one was open for 0% of the time, Pallas kernels for 0%

profile of v3, /device:TPU:33, one launch (start us, length us, event | category | flops | bytes accessed | tf_op | source)
XLA Modules:
  0.0 89.3 jit_solution(13053349045529003476)
XLA Ops:
  0.0 0.0 copy-start
  0.0 1.6 %shard_map.46 = bf16[32,8,512]{2,1,0:T(8,128)(2,1)} custom-call(s32[4]{0:T(128)} %plan_ref.1, bf16[4,2,512]{2,1,0:T(2,128)(2,1)} %inputs_ref.1, bf16[4,2,512]{2,1,0:T(2,128)(2,1)} %cotangent_ref.1), custom_call_target="tpu_custom_call" | custom-call | tf_op jit(solution)/shard_map/pallas_call | solution.py:31
  1.6 14.0 %all-to-all-start = ((bf16[32,8,512]{2,1,0:T(8,128)(2,1)}), bf16[32,8,512]{2,1,0:T(8,128)(2,1)S(1)}, u32[]{:S(2)}, u32[]{:S(2)}) async-start(bf16[32,8,512]{2,1,0:T(8,128)(2,1)} %shard_map.46), calls=%async_computation | async-start | bytes 524288 | tf_op jit(solution)/shard_map/all_to_all | solution.py:52
  15.6 10.8 %all-to-all-done = bf16[32,8,512]{2,1,0:T(8,128)(2,1)S(1)} async-done(((bf16[32,8,512]{2,1,0:T(8,128)(2,1)}), bf16[32,8,512]{2,1,0:T(8,128)(2,1)S(1)}, u32[]{:S(2)}, u32[]{:S(2)}) %all-to-all-start) | async-done | bytes 262176 | tf_op jit(solution)/shard_map/all_to_all | solution.py:52
  26.4 0.0 copy-done
  26.4 0.7 convolution_convert_fusion.1
  27.1 6.3 %collective-permute-start = (bf16[128,1664]{1,0:T(8,128)(2,1)S(1)}, bf16[128,1664]{1,0:T(8,128)(2,1)S(1)}, u32[]{:S(2)}, u32[]{:S(2)}) collective-permute-start(bf16[128,1664]{1,0:T(8,128)(2,1)S(1)} %convolution_convert_fusion.1), channel_id=1, source_target_pairs={{0,1},{1,0},{2,3},{3,2},{4,5},{5,4},{6,7},{7,6},{8,9},{9,8},{10,11... | collective-permute-start | bytes 1277960 | tf_op jit(solution)/shard_map/ppermute | solution.py:63
  33.4 1.4 %collective-permute-done = bf16[128,1664]{1,0:T(8,128)(2,1)S(1)} collective-permute-done((bf16[128,1664]{1,0:T(8,128)(2,1)S(1)}, bf16[128,1664]{1,0:T(8,128)(2,1)S(1)}, u32[]{:S(2)}, u32[]{:S(2)}) %collective-permute-start) | collective-permute-done | bytes 426016 | tf_op jit(solution)/shard_map/ppermute | solution.py:63
  34.8 0.7 add_convert_fusion
  35.5 14.8 %all_to_all.15 = bf16[8,16,1664]{2,1,0:T(8,128)(2,1)S(1)} all-to-all(bf16[8,16,1664]{2,1,0:T(8,128)(2,1)S(1)} %bitcast.24), channel_id=1, replica_groups=mesh['half'=2,'yl'=2,'zl'=8,'zh'=2,'x'=4,'core'=2] {'half','x'}, dimensions={0} | all-to-all | bytes 851968 | tf_op jit(solution)/shard_map/all_to_all | solution.py:66
  50.3 0.1 bitcast_reduce_fusion
  50.3 9.6 %collective-permute-start.1 = (bf16[2,16,1664]{2,1,0:T(8,128)(2,1)S(1)}, bf16[2,16,1664]{2,1,0:T(8,128)(2,1)S(1)}, u32[]{:S(2)}, u32[]{:S(2)}) collective-permute-start(bf16[2,16,1664]{2,1,0:T(8,128)(2,1)S(1)} %bitcast_reduce_fusion), channel_id=1, source_target_pairs={{0,8},{8,0},{1,9},{9,1},{2,10},{10,2},{3,11},{11,3},{4,12},{12,4},... | collective-permute-start | bytes 319496 | tf_op jit(solution)/shard_map/ppermute | solution.py:69
  59.9 8.4 %collective-permute-done.1 = bf16[2,16,1664]{2,1,0:T(8,128)(2,1)S(1)} collective-permute-done((bf16[2,16,1664]{2,1,0:T(8,128)(2,1)S(1)}, bf16[2,16,1664]{2,1,0:T(8,128)(2,1)S(1)}, u32[]{:S(2)}, u32[]{:S(2)}) %collective-permute-start.1) | collective-permute-done | bytes 106528 | tf_op jit(solution)/shard_map/ppermute | solution.py:69
  68.3 0.1 fusion.11
  68.5 10.9 %all_to_all.16 = bf16[8,16,1664]{2,1,0:T(8,128)(2,1)S(1)} all-to-all(bf16[8,16,1664]{2,1,0:T(8,128)(2,1)S(1)} %pad_maximum_fusion), channel_id=1, replica_groups=mesh['half'=2,'yl'=2,'zl'=8,'zh'=2,'x'=4,'core'=2] {'half','x'}, dimensions={0} | all-to-all | bytes 851968 | tf_op jit(solution)/shard_map/all_to_all | solution.py:83
  79.4 6.7 %collective-permute-start.2 = (bf16[128,1664]{1,0:T(8,128)(2,1)S(1)}, bf16[128,1664]{1,0:T(8,128)(2,1)S(1)}, u32[]{:S(2)}, u32[]{:S(2)}) collective-permute-start(bf16[128,1664]{1,0:T(8,128)(2,1)S(1)} %bitcast.26), channel_id=1, source_target_pairs={{0,1},{1,0},{2,3},{3,2},{4,5},{5,4},{6,7},{7,6},{8,9},{9,8},{10,11... | collective-permute-start | bytes 1277960 | tf_op jit(solution)/shard_map/ppermute | solution.py:84
  86.1 1.4 %collective-permute-done.2 = bf16[128,1664]{1,0:T(8,128)(2,1)S(1)} collective-permute-done((bf16[128,1664]{1,0:T(8,128)(2,1)S(1)}, bf16[128,1664]{1,0:T(8,128)(2,1)S(1)}, u32[]{:S(2)}, u32[]{:S(2)}) %collective-permute-start.2) | collective-permute-done | bytes 426016 | tf_op jit(solution)/shard_map/ppermute | solution.py:84
  87.4 1.8 %fusion = bf16[1,1664,512]{2,1,0:T(8,128)(2,1)} fusion(bf16[128,1664]{1,0:T(8,128)(2,1)S(1)} %collective-permute-done.2, bf16[128,1664]{1,0:T(8,128)(2,1)S(1)} %bitcast.27, bf16[128,512]{1,0:T(8,128)(2,1)S(1)} %get-tuple-element.5, bf16[128,512]{1,0:T(8,128)(2,1)S(1)} %get-tuple-element.6), kind=kOutput, calls=%fused_computation.1 | convolution fusion | flops 439287808 | bytes 2818048 | tf_op jit(solution)/shard_map/rf,rd->fd/dot_general | solution.py:85
  (5 shorter events, 0.1 us)
Async XLA Ops:
  0.0 26.4 %copy-start = (bf16[1,1664,512]{2,1,0:T(8,128)(2,1)S(1)}, bf16[1,1664,512]{2,1,0:T(8,128)(2,1)}, u32[]{:S(2)}) copy-start(bf16[1,1664,512]{2,1,0:T(8,128)(2,1)} %param.7) | copy-start | bytes 5111812
  1.6 24.8 %all-to-all-start = ((bf16[32,8,512]{2,1,0:T(8,128)(2,1)}), bf16[32,8,512]{2,1,0:T(8,128)(2,1)S(1)}, u32[]{:S(2)}, u32[]{:S(2)}) async-start(bf16[32,8,512]{2,1,0:T(8,128)(2,1)} %shard_map.46), calls=%async_computation | async-start | bytes 524288 | tf_op jit(solution)/shard_map/all_to_all | solution.py:52
  27.1 7.7 %collective-permute-start = (bf16[128,1664]{1,0:T(8,128)(2,1)S(1)}, bf16[128,1664]{1,0:T(8,128)(2,1)S(1)}, u32[]{:S(2)}, u32[]{:S(2)}) collective-permute-start(bf16[128,1664]{1,0:T(8,128)(2,1)S(1)} %convolution_convert_fusion.1), channel_id=1, source_target_pairs={{0,1},{1,0},{2,3},{3,2},{4,5},{5,4},{6,7},{7,6},{8,9},{9,8},{10,11... | collective-permute-start | bytes 1277960 | tf_op jit(solution)/shard_map/ppermute | solution.py:63
  50.3 17.9 %collective-permute-start.1 = (bf16[2,16,1664]{2,1,0:T(8,128)(2,1)S(1)}, bf16[2,16,1664]{2,1,0:T(8,128)(2,1)S(1)}, u32[]{:S(2)}, u32[]{:S(2)}) collective-permute-start(bf16[2,16,1664]{2,1,0:T(8,128)(2,1)S(1)} %bitcast_reduce_fusion), channel_id=1, source_target_pairs={{0,8},{8,0},{1,9},{9,1},{2,10},{10,2},{3,11},{11,3},{4,12},{12,4},... | collective-permute-start | bytes 319496 | tf_op jit(solution)/shard_map/ppermute | solution.py:69
  79.4 8.1 %collective-permute-start.2 = (bf16[128,1664]{1,0:T(8,128)(2,1)S(1)}, bf16[128,1664]{1,0:T(8,128)(2,1)S(1)}, u32[]{:S(2)}, u32[]{:S(2)}) collective-permute-start(bf16[128,1664]{1,0:T(8,128)(2,1)S(1)} %bitcast.26), channel_id=1, source_target_pairs={{0,1},{1,0},{2,3},{3,2},{4,5},{5,4},{6,7},{7,6},{8,9},{9,8},{10,11... | collective-permute-start | bytes 1277960 | tf_op jit(solution)/shard_map/ppermute | solution.py:84

commit v4 on v2

--- a/solution.py
+++ b/solution.py
@@ -9,6 +9,7 @@
 SECTION = ("half", "yl", "zl")
 TENSOR = ("zh", "x", "core")
 OWNERS = ("half", "x")
+TILES = 4
 
 
 def pack_kernel(plan_ref, inputs_ref, cotangent_ref, out_ref):
@@ -39,33 +40,77 @@
     )(plan, inputs, cotangent)
 
 
+def gradient_kernel(side_ref, left_ref, rows_ref, *refs):
+    out_ref = refs[-1]
+    tile = out_ref.shape[1]
+    first = pl.multiple_of(pl.program_id(0) * tile, tile)
+    out_ref[0] = jnp.dot(
+        left_ref[pl.ds(first, tile), :], rows_ref[...], preferred_element_type=jnp.float32
+    ).astype(out_ref.dtype)
+
+
+def gradient(side, left, rows, done=None):
+    units, row_count = left.shape
+    width = rows.shape[1]
+    tile = units // TILES
+    operands = (side, left, rows) + (() if done is None else (done,))
+    return pl.pallas_call(
+        gradient_kernel,
+        out_shape=jax.ShapeDtypeStruct((2, units, width), left.dtype),
+        grid_spec=pltpu.PrefetchScalarGridSpec(
+            num_scalar_prefetch=1,
+            grid=(TILES,),
+            in_specs=[
+                pl.BlockSpec(memory_space=pltpu.VMEM),
+                pl.BlockSpec(memory_space=pltpu.VMEM),
+            ]
+            + ([] if done is None else [pl.BlockSpec(memory_space=pl.ANY)]),
+            out_specs=pl.BlockSpec((1, tile, width), lambda i, side_ref: (side_ref[0], i, 0)),
+        ),
+        input_output_aliases={} if done is None else {3: 0},
+        cost_estimate=pl.CostEstimate(
+            flops=2 * units * row_count * width,
+            bytes_accessed=2 * units * (row_count + width),
+            transcendentals=0,
+        ),
+    )(*operands)
+
+
 def local(inputs, cotangent, plan, weights):
-    piece = weights[0]
-    hidden_units, width = piece.shape
+    hidden_units, width = weights.shape[1:]
     sections = lax.axis_size(SECTION)
+    depth = lax.axis_size("zl")
     owners = lax.axis_size(OWNERS)
     core = lax.axis_index("core")
     twin = [(0, 1), (1, 0)]
 
-    rows = lax.all_to_all(pack(plan, inputs, cotangent, sections), SECTION, 0, 0)
-    rows = rows.reshape(2, -1, width)
-    half_rows = rows.shape[1]
-    rows_here = lax.dynamic_index_in_dim(rows, core, 0, keepdims=False)
-    rows_there = lax.dynamic_index_in_dim(rows, 1 - core, 0, keepdims=False)
+    order = [
+        first + (z + depth // 2) % depth for first in range(0, sections, depth) for z in range(depth)
+    ]
+    rows = lax.all_to_all(
+        pack(plan, inputs, cotangent, sections), SECTION, 0, 0, axis_index_groups=[order]
+    ).reshape(-1, width)
+    row_count = rows.shape[0]
 
-    def project(values):
-        return jnp.einsum("rd,fd->rf", values, piece, preferred_element_type=jnp.float32).astype(
-            jnp.bfloat16
-        )
+    piece = weights.reshape(2, hidden_units // 2, width)
+    piece_own = lax.dynamic_index_in_dim(piece, core, 0, keepdims=False)
+    piece_twin = lax.ppermute(
+        lax.dynamic_index_in_dim(piece, 1 - core, 0, keepdims=False), "core", twin
+    )
+    rows_twin = lax.ppermute(rows, "core", twin)
 
-    arrived = lax.ppermute(project(rows_there), "core", twin)
-    partial = project(rows_here).astype(jnp.float32) + arrived.astype(jnp.float32)
-    partial = partial.astype(jnp.bfloat16).reshape(owners, half_rows // owners, hidden_units)
+    def project(values, matrix):
+        return jnp.einsum("fd,rd->fr", matrix, values, preferred_element_type=jnp.float32)
+
+    near_part = lax.optimization_barrier(project(rows, piece_own).astype(jnp.bfloat16))
+    far_part = lax.optimization_barrier(project(rows_twin, piece_twin).astype(jnp.bfloat16))
+    partial = near_part.astype(jnp.float32) + far_part.astype(jnp.float32)
+    partial = partial.astype(jnp.bfloat16).reshape(owners, -1, row_count)
     gathered = lax.all_to_all(partial, OWNERS, 0, 0)
     gathered = gathered.reshape((2, owners // 2) + gathered.shape[1:])
     near = jnp.sum(gathered.astype(jnp.float32), axis=1).astype(jnp.bfloat16)
-    far = lax.ppermute(near, "zh", twin)
-    total = near.astype(jnp.float32) + far.astype(jnp.float32)
+    both = lax.all_gather(near, "zh")
+    total = both[0].astype(jnp.float32) + both[1].astype(jnp.float32)
     pre_sum = total[0]
     grad_hidden = total[1].astype(jnp.bfloat16).astype(jnp.float32)
     logistic = jax.nn.sigmoid(pre_sum)
@@ -78,15 +123,11 @@
             jnp.broadcast_to(hidden[None], (owners // 2,) + hidden.shape),
         ]
     )
-    left_here = lax.all_to_all(answer, OWNERS, 0, 0).reshape(half_rows, hidden_units)
-    left_there = lax.ppermute(left_here, "core", twin)
-    grads = jnp.einsum(
-        "rf,rd->fd",
-        jnp.concatenate([left_here, left_there]),
-        jnp.concatenate([rows_here, rows_there]),
-        preferred_element_type=jnp.float32,
-    )
-    return grads.astype(jnp.bfloat16)[None]
+    left = lax.all_to_all(answer, OWNERS, 0, 0).reshape(-1, row_count)
+    whole = lax.all_gather(left, "core", axis=0, tiled=True)
+    grads = jnp.einsum("fr,rd->fd", whole, rows, preferred_element_type=jnp.float32)
+    grads = grads.astype(jnp.bfloat16)
+    return grads.reshape(1, hidden_units, width)
 
 
 def solution(mesh):

time: 96.2 us -> 86 us (0.89)
  the two profiles are of different devices: /device:TPU:1 before, /device:TPU:33 now
where the time goes in v4:
time: 86 us; the launch traced here: 85.6 us
  blocking collectives  49.2 us (57%)
  starting transfers between devices  23.4 us (27%)
  waiting for transfers between devices  7.39 us (9%)
  matrix products  2.6 us (3%)
  Pallas kernels  1.57 us (2%)
  local copies, waits for them, and re-layouts  1 us (1%)
    all_gather x1, blocking collectives, local(): both = lax.all_gather(near, 'zh')  16.7 us
    all_to_all x1, blocking collectives, local(): gathered = lax.all_to_all(partial, OWNERS, 0, 0)  14.8 us
    all_to_all x1, starting transfers between devices, local(): lax.all_to_all(pack(plan, inputs, cotangent, sections), SECTION, 0, 0, ax...  14 us
    all_to_all x1, blocking collectives, local(): left = lax.all_to_all(answer, OWNERS, 0, 0).reshape(-1, row_count)  10.9 us
    all_gather x1, blocking collectives, local(): whole = lax.all_gather(left, 'core', axis=0, tiled=True)  6.82 us
    all_to_all x1, waiting for transfers between devices, local(): lax.all_to_all(pack(plan, inputs, cotangent, sections), SECTION, 0, 0, ax...  6.67 us
    ppermute x1, starting transfers between devices, local(): rows_twin = lax.ppermute(rows, 'core', twin)  6.33 us
    ppermute x1, starting transfers between devices, local(): lax.ppermute(lax.dynamic_index_in_dim(piece, 1 - core, 0, keepdims=False)...  3.13 us
  transfers between devices with their start and end apart: 3, of which 2 were waited for; matrix products, arithmetic and copies ran while one was open for 2% of the time, Pallas kernels for 0%

profile of v4, /device:TPU:33, one launch (start us, length us, event | category | flops | bytes accessed | tf_op | source)
XLA Modules:
  0.0 85.6 jit_solution(14527999716418765438)
XLA Ops:
  0.0 0.0 copy-start
  0.0 1.6 %shard_map.46 = bf16[32,8,512]{2,1,0:T(8,128)(2,1)} custom-call(s32[4]{0:T(128)} %plan_ref.1, bf16[4,2,512]{2,1,0:T(2,128)(2,1)} %inputs_ref.1, bf16[4,2,512]{2,1,0:T(2,128)(2,1)} %cotangent_ref.1), custom_call_target="tpu_custom_call" | custom-call | tf_op jit(solution)/shard_map/pallas_call | solution.py:31
  1.6 14.0 %all-to-all-start = ((bf16[32,8,512]{2,1,0:T(8,128)(2,1)}), bf16[32,8,512]{2,1,0:T(8,128)(2,1)S(1)}, u32[]{:S(2)}, u32[]{:S(2)}) async-start(bf16[32,8,512]{2,1,0:T(8,128)(2,1)} %shard_map.46), calls=%async_computation | async-start | bytes 524288 | tf_op jit(solution)/shard_map/all_to_all | solution.py:90
  15.5 0.0 copy-done
  15.6 1.0 %dynamic-slice_bitcast_fusion = bf16[832,512]{1,0:T(8,128)(2,1)} fusion(bf16[2,832,512]{2,1,0:T(8,128)(2,1)S(1)} %bitcast.44, s32[]{:T(128)S(6)} %select_n.8), kind=kLoop, calls=%fused_computation.6 | loop fusion | bytes 1703940 | tf_op jit(solution)/shard_map/jit(dynamic_index_in_dim)/squeeze | solution.py:98
  16.5 3.1 %collective-permute-start = (bf16[832,512]{1,0:T(8,128)(2,1)}, bf16[832,512]{1,0:T(8,128)(2,1)S(1)}, u32[]{:S(2)}, u32[]{:S(2)}) collective-permute-start(bf16[832,512]{1,0:T(8,128)(2,1)} %dynamic-slice_bitcast_fusion), channel_id=1, source_target_pairs={{0,1},{1,0},{2,3},{3,2},{4,5},{5,4},{6,7},{7,6},{8,9},{9,8},{10,11... | collective-permute-start | bytes 2555912 | tf_op jit(solution)/shard_map/ppermute | solution.py:97
  19.7 6.7 %all-to-all-done = bf16[32,8,512]{2,1,0:T(8,128)(2,1)S(1)} async-done(((bf16[32,8,512]{2,1,0:T(8,128)(2,1)}), bf16[32,8,512]{2,1,0:T(8,128)(2,1)S(1)}, u32[]{:S(2)}, u32[]{:S(2)}) %all-to-all-start) | async-done | bytes 262176 | tf_op jit(solution)/shard_map/all_to_all | solution.py:90
  26.3 6.3 %collective-permute-start.1 = (bf16[256,512]{1,0:T(8,128)(2,1)S(1)}, bf16[256,512]{1,0:T(8,128)(2,1)S(1)}, u32[]{:S(2)}, u32[]{:S(2)}) collective-permute-start(bf16[256,512]{1,0:T(8,128)(2,1)S(1)} %bitcast.45), channel_id=1, source_target_pairs={{0,1},{1,0},{2,3},{3,2},{4,5},{5,4},{6,7},{7,6},{8,9},{9,8},{10,11... | collective-permute-start | bytes 786440 | tf_op jit(solution)/shard_map/ppermute | solution.py:100
  32.7 0.4 convolution_convert_fusion.2
  33.1 0.0 collective-permute-done
  33.1 0.7 collective-permute-done.1
  33.8 0.4 convolution_convert_fusion.1
  34.2 0.1 add_convert_fusion
  34.3 14.8 %all_to_all.15 = bf16[8,104,256]{2,1,0:T(8,128)(2,1)S(1)} all-to-all(bf16[8,104,256]{2,1,0:T(8,128)(2,1)S(1)} %bitcast.46), channel_id=1, replica_groups=mesh['half'=2,'yl'=2,'zl'=8,'zh'=2,'x'=4,'core'=2] {'half','x'}, dimensions={0} | all-to-all | bytes 851968 | tf_op jit(solution)/shard_map/all_to_all | solution.py:109
  49.1 0.1 bitcast_reduce_fusion
  49.2 16.7 %all-gather = bf16[4,104,256]{2,1,0:T(8,128)(2,1)S(1)} all-gather(bf16[2,104,256]{2,1,0:T(8,128)(2,1)S(1)} %bitcast_reduce_fusion), channel_id=2, replica_groups=mesh['half'=2,'yl'=2,'zl'=8,'zh'=2,'x'=4,'core'=2] {'zh'}, dimensions={0}, use_global_device_ids=true | all-gather | bytes 319488 | tf_op jit(solution)/shard_map/all_gather | solution.py:112
  66.1 10.9 %all_to_all.16 = bf16[8,104,256]{2,1,0:T(8,128)(2,1)S(1)} all-to-all(bf16[8,104,256]{2,1,0:T(8,128)(2,1)S(1)} %pad_maximum_fusion), channel_id=1, replica_groups=mesh['half'=2,'yl'=2,'zl'=8,'zh'=2,'x'=4,'core'=2] {'half','x'}, dimensions={0} | all-to-all | bytes 851968 | tf_op jit(solution)/shard_map/all_to_all | solution.py:126
  77.0 6.8 %all_gather.11 = bf16[1664,256]{1,0:T(8,128)(2,1)S(1)} all-gather(bf16[832,256]{1,0:T(8,128)(2,1)S(1)} %bitcast.47), channel_id=1, replica_groups=mesh['half'=2,'yl'=2,'zl'=8,'zh'=2,'x'=4,'core'=2] {'core'}, dimensions={0}, use_global_device_ids=true | all-gather | bytes 1277952 | tf_op jit(solution)/shard_map/all_gather | solution.py:127
  83.8 1.8 %fusion = bf16[1,1664,512]{2,1,0:T(8,128)(2,1)} fusion(bf16[1664,256]{1,0:T(8,128)(2,1)S(1)} %all_gather.11, bf16[32,8,512]{2,1,0:T(8,128)(2,1)S(1)} %all-to-all-done), kind=kOutput, calls=%fused_computation.1 | convolution fusion | flops 437059584 | bytes 2818048 | tf_op jit(solution)/shard_map/fr,rd->fd/dot_general | solution.py:128
  (5 shorter events, 0.1 us)
Async XLA Ops:
  0.0 15.5 %copy-start = (bf16[1,1664,512]{2,1,0:T(8,128)(2,1)S(1)}, bf16[1,1664,512]{2,1,0:T(8,128)(2,1)}, u32[]{:S(2)}) copy-start(bf16[1,1664,512]{2,1,0:T(8,128)(2,1)} %param.7) | copy-start | bytes 5111812
  1.6 24.8 %all-to-all-start = ((bf16[32,8,512]{2,1,0:T(8,128)(2,1)}), bf16[32,8,512]{2,1,0:T(8,128)(2,1)S(1)}, u32[]{:S(2)}, u32[]{:S(2)}) async-start(bf16[32,8,512]{2,1,0:T(8,128)(2,1)} %shard_map.46), calls=%async_computation | async-start | bytes 524288 | tf_op jit(solution)/shard_map/all_to_all | solution.py:90
  16.5 16.6 %collective-permute-start = (bf16[832,512]{1,0:T(8,128)(2,1)}, bf16[832,512]{1,0:T(8,128)(2,1)S(1)}, u32[]{:S(2)}, u32[]{:S(2)}) collective-permute-start(bf16[832,512]{1,0:T(8,128)(2,1)} %dynamic-slice_bitcast_fusion), channel_id=1, source_target_pairs={{0,1},{1,0},{2,3},{3,2},{4,5},{5,4},{6,7},{7,6},{8,9},{9,8},{10,11... | collective-permute-start | bytes 2555912 | tf_op jit(solution)/shard_map/ppermute | solution.py:97
  26.3 7.5 %collective-permute-start.1 = (bf16[256,512]{1,0:T(8,128)(2,1)S(1)}, bf16[256,512]{1,0:T(8,128)(2,1)S(1)}, u32[]{:S(2)}, u32[]{:S(2)}) collective-permute-start(bf16[256,512]{1,0:T(8,128)(2,1)S(1)} %bitcast.45), channel_id=1, source_target_pairs={{0,1},{1,0},{2,3},{3,2},{4,5},{5,4},{6,7},{7,6},{8,9},{9,8},{10,11... | collective-permute-start | bytes 786440 | tf_op jit(solution)/shard_map/ppermute | solution.py:100

commit v5 on v4

v5 whole, which is shorter than its diff:
```python
import jax
import jax.numpy as jnp
import numpy as np
from jax import lax
from jax.experimental import pallas as pl
from jax.experimental.pallas import tpu as pltpu
from jax.sharding import Mesh, PartitionSpec as P

SECTION = ("half", "yl", "zl")
TENSOR = ("zh", "x", "core")
OWNERS = ("half", "x")
TILES = 4


def pack_kernel(plan_ref, inputs_ref, cotangent_ref, out_ref):
    batches = inputs_ref.shape[0]
    half = out_ref.shape[0] // 2
    returning = jnp.concatenate(
        [cotangent_ref[k].astype(jnp.float32) for k in range(batches)], axis=0
    ).astype(out_ref.dtype)
    entering = jnp.concatenate(
        [inputs_ref[plan_ref[k]].astype(jnp.float32) for k in range(batches)], axis=0
    ).astype(out_ref.dtype)
    for i in range(half):
        out_ref[i] = returning
        out_ref[half + i] = entering


def pack(plan, inputs, cotangent, sections):
    batches, tokens, width = inputs.shape
    return pl.pallas_call(
        pack_kernel,
        out_shape=jax.ShapeDtypeStruct((sections, batches * tokens, width), inputs.dtype),
        in_specs=[
            pl.BlockSpec(memory_space=pltpu.SMEM),
            pl.BlockSpec(memory_space=pltpu.VMEM),
            pl.BlockSpec(memory_space=pltpu.VMEM),
        ],
        out_specs=pl.BlockSpec(memory_space=pltpu.VMEM),
    )(plan, inputs, cotangent)


def gradient_kernel(left_ref, rows_ref, out_ref, held_ref, sems):
    tile = left_ref.shape[0] // 4
    copies = []
    for i in range(4):
        block = pl.ds(i * tile, tile)
        held_ref[block, :] = jnp.dot(
            left_ref[block, :], rows_ref[...], preferred_element_type=jnp.float32
        ).astype(held_ref.dtype)
        copies.append(pltpu.make_async_copy(held_ref.at[block], out_ref.at[block], sems.at[i]))
        copies[-1].start()
    for copy in copies:
        copy.wait()


def gradient(left, rows):
    units = left.shape[0]
    width = rows.shape[1]
    return pl.pallas_call(
        gradient_kernel,
        out_shape=jax.ShapeDtypeStruct((units, width), left.dtype),
        in_specs=[pl.BlockSpec(memory_space=pltpu.VMEM), pl.BlockSpec(memory_space=pltpu.VMEM)],
        out_specs=pl.BlockSpec(memory_space=pl.ANY),
        scratch_shapes=[pltpu.VMEM((units, width), left.dtype), pltpu.SemaphoreType.DMA((4,))],
        compiler_params=pltpu.CompilerParams(vmem_limit_bytes=8 << 20),
    )(left, rows)


def local(inputs, cotangent, plan, weights):
    hidden_units, width = weights.shape[1:]
    sections = lax.axis_size(SECTION)
    depth = lax.axis_size("zl")
    owners = lax.axis_size(OWNERS)
    core = lax.axis_index("core")
    twin = [(0, 1), (1, 0)]

    order = [
        first + (z + depth // 2) % depth
        for first in (*range(sections // 2, sections, depth), *range(0, sections // 2, depth))
        for z in range(depth)
    ]
    owner_order = list(range(owners))[::-1]
    rows = lax.all_to_all(
        pack(plan, inputs, cotangent, sections), SECTION, 0, 0, axis_index_groups=[order]
    ).reshape(-1, width)
    row_count = rows.shape[0]

    piece = weights.reshape(2, hidden_units // 2, width)
    piece_own = lax.dynamic_index_in_dim(piece, core, 0, keepdims=False)
    piece_twin = lax.ppermute(
        lax.dynamic_index_in_dim(piece, 1 - core, 0, keepdims=False), "core", twin
    )
    rows_twin = lax.ppermute(rows, "core", twin)

    def project(values, matrix):
        return jnp.einsum("fd,rd->fr", matrix, values, preferred_element_type=jnp.float32)

    near_part = lax.optimization_barrier(project(rows, piece_own).astype(jnp.bfloat16))
    far_part = lax.optimization_barrier(project(rows_twin, piece_twin).astype(jnp.bfloat16))
    partial = near_part.astype(jnp.float32) + far_part.astype(jnp.float32)
    partial = partial.astype(jnp.bfloat16).reshape(owners, -1, row_count)
    gathered = lax.all_to_all(partial, OWNERS, 0, 0, axis_index_groups=[owner_order])
    gathered = gathered.reshape((2, owners // 2) + gathered.shape[1:])
    near = jnp.sum(gathered.astype(jnp.float32), axis=1).astype(jnp.bfloat16)
    both = lax.all_gather(near, "zh")
    total = both[0].astype(jnp.float32) + both[1].astype(jnp.float32)
    pre_sum = total[1]
    grad_hidden = total[0].astype(jnp.bfloat16).astype(jnp.float32)
    logistic = jax.nn.sigmoid(pre_sum)
    hidden = (pre_sum * logistic).astype(jnp.bfloat16)
    grad_pre = (grad_hidden * logistic * (1.0 + pre_sum * (1.0 - logistic))).astype(jnp.bfloat16)

    answer = jnp.concatenate(
        [
            jnp.broadcast_to(hidden[None], (owners // 2,) + hidden.shape),
            jnp.broadcast_to(grad_pre[None], (owners // 2,) + grad_pre.shape),
        ]
    )
    left = lax.all_to_all(answer, OWNERS, 0, 0, axis_index_groups=[owner_order]).reshape(-1, row_count)
    whole = lax.all_gather(left, "core", axis=0, tiled=True)
    grads = gradient(whole, rows)
    return grads.reshape(1, hidden_units, width)


def solution(mesh):
    fine = Mesh(
        np.asarray(mesh.devices).reshape(2, 2, 8, 2, 4, 2),
        ("half", "yl", "zl", "zh", "x", "core"),
    )
    placed = (
        P(None, SECTION, TENSOR),
        P(None, SECTION, TENSOR),
        P(),
        P(SECTION, None, TENSOR),
    )
    return jax.shard_map(
        local, mesh=fine, in_specs=placed, out_specs=P(SECTION, None, TENSOR), check_vma=False
    )
```

time: 86 us -> 83.9 us (0.976)
  matrix products: 2.6 us -> 0.83 us
  starting transfers between devices: 23.4 us -> 21.7 us
  Pallas kernels: 1.57 us -> 3.05 us
    all_to_all x2, blocking collectives: 25.7 us -> 28.6 us  [the longest x1 15 us: local(): lax.all_to_all(answer, OWNERS, 0, 0, axis_index_groups=[owner_order])]
    all_gather x1, blocking collectives: 6.82 us -> 3.95 us  [local(): whole = lax.all_gather(left, 'core', axis=0, tiled=True)]
    ppermute x1, starting transfers between devices: 6.33 us -> 3.85 us  [local(): rows_twin = lax.ppermute(rows, 'core', twin)]
    dot_general x1 -> x0, matrix products: 1.78 us -> none  [local(): jnp.einsum('fr,rd->fd', whole, rows, preferred_element_type=jnp.float32)]
    pallas_call x0 -> x1, Pallas kernels: none -> 1.49 us  [gradient(): pl.pallas_call(gradient_kernel, out_shape=jax.ShapeDtypeStruct((units, wi...]
where the time goes in v5:
time: 83.9 us; the launch traced here: 83.5 us
  blocking collectives  49.2 us (59%)
  starting transfers between devices  21.7 us (26%)
  waiting for transfers between devices  7.36 us (9%)
  Pallas kernels  3.05 us (4%)
  local copies, waits for them, and re-layouts  1 us (1%)
    all_gather x1, blocking collectives, local(): both = lax.all_gather(near, 'zh')  16.6 us
    all_to_all x1, blocking collectives, local(): lax.all_to_all(answer, OWNERS, 0, 0, axis_index_groups=[owner_order])  15 us
    all_to_all x1, starting transfers between devices, local(): lax.all_to_all(pack(plan, inputs, cotangent, sections), SECTION, 0, 0, ax...  14.7 us
    all_to_all x1, blocking collectives, local(): lax.all_to_all(partial, OWNERS, 0, 0, axis_index_groups=[owner_order])  13.7 us
    all_to_all x1, waiting for transfers between devices, local(): lax.all_to_all(pack(plan, inputs, cotangent, sections), SECTION, 0, 0, ax...  6.65 us
    all_gather x1, blocking collectives, local(): whole = lax.all_gather(left, 'core', axis=0, tiled=True)  3.95 us
    ppermute x1, starting transfers between devices, local(): rows_twin = lax.ppermute(rows, 'core', twin)  3.85 us
    ppermute x1, starting transfers between devices, local(): lax.ppermute(lax.dynamic_index_in_dim(piece, 1 - core, 0, keepdims=False)...  3.13 us
  transfers between devices with their start and end apart: 3, of which 2 were waited for; matrix products, arithmetic and copies ran while one was open for 2% of the time, Pallas kernels for 0%

profile of v5, /device:TPU:33, one launch (start us, length us, event | category | flops | bytes accessed | tf_op | source)
XLA Modules:
  0.0 83.5 jit_solution(10563442799929852233)
XLA Ops:
  0.0 0.0 copy-start
  0.0 1.6 %shard_map.46 = bf16[32,8,512]{2,1,0:T(8,128)(2,1)} custom-call(s32[4]{0:T(128)} %plan_ref.1, bf16[4,2,512]{2,1,0:T(2,128)(2,1)} %inputs_ref.1, bf16[4,2,512]{2,1,0:T(2,128)(2,1)} %cotangent_ref.1), custom_call_target="tpu_custom_call" | custom-call | tf_op jit(solution)/shard_map/pallas_call | solution.py:31
  1.6 14.7 %all-to-all-start = ((bf16[32,8,512]{2,1,0:T(8,128)(2,1)}), bf16[32,8,512]{2,1,0:T(8,128)(2,1)S(1)}, u32[]{:S(2)}, u32[]{:S(2)}) async-start(bf16[32,8,512]{2,1,0:T(8,128)(2,1)} %shard_map.46), calls=%async_computation | async-start | bytes 524288 | tf_op jit(solution)/shard_map/all_to_all | solution.py:84
  16.3 0.0 copy-done
  16.3 1.0 %dynamic-slice_bitcast_fusion = bf16[832,512]{1,0:T(8,128)(2,1)} fusion(bf16[2,832,512]{2,1,0:T(8,128)(2,1)S(1)} %bitcast.40, s32[]{:T(128)S(6)} %select_n.8), kind=kLoop, calls=%fused_computation.4 | loop fusion | bytes 1703940 | tf_op jit(solution)/shard_map/jit(dynamic_index_in_dim)/squeeze | solution.py:92
  17.3 3.1 %collective-permute-start = (bf16[832,512]{1,0:T(8,128)(2,1)}, bf16[832,512]{1,0:T(8,128)(2,1)S(1)}, u32[]{:S(2)}, u32[]{:S(2)}) collective-permute-start(bf16[832,512]{1,0:T(8,128)(2,1)} %dynamic-slice_bitcast_fusion), channel_id=1, source_target_pairs={{0,1},{1,0},{2,3},{3,2},{4,5},{5,4},{6,7},{7,6},{8,9},{9,8},{10,11... | collective-permute-start | bytes 2555912 | tf_op jit(solution)/shard_map/ppermute | solution.py:91
  20.4 6.7 %all-to-all-done = bf16[32,8,512]{2,1,0:T(8,128)(2,1)S(1)} async-done(((bf16[32,8,512]{2,1,0:T(8,128)(2,1)}), bf16[32,8,512]{2,1,0:T(8,128)(2,1)S(1)}, u32[]{:S(2)}, u32[]{:S(2)}) %all-to-all-start) | async-done | bytes 262176 | tf_op jit(solution)/shard_map/all_to_all | solution.py:84
  27.1 3.8 %collective-permute-start.1 = (bf16[256,512]{1,0:T(8,128)(2,1)S(1)}, bf16[256,512]{1,0:T(8,128)(2,1)S(1)}, u32[]{:S(2)}, u32[]{:S(2)}) collective-permute-start(bf16[256,512]{1,0:T(8,128)(2,1)S(1)} %bitcast.41), channel_id=1, source_target_pairs={{0,1},{1,0},{2,3},{3,2},{4,5},{5,4},{6,7},{7,6},{8,9},{9,8},{10,11... | collective-permute-start | bytes 786440 | tf_op jit(solution)/shard_map/ppermute | solution.py:94
  30.9 0.4 convolution_convert_fusion.1
  31.3 0.0 collective-permute-done
  31.3 0.7 collective-permute-done.1
  32.0 0.4 convolution_convert_fusion
  32.5 0.1 add_convert_fusion
  32.6 13.7 %all_to_all.15 = bf16[8,104,256]{2,1,0:T(8,128)(2,1)S(1)} all-to-all(bf16[8,104,256]{2,1,0:T(8,128)(2,1)S(1)} %bitcast.43), channel_id=1, replica_groups={{262,260,258,256,6,4,2,0},{263,261,259,257,7,5,3,1},{270,268,266,264,14..., dimensions={0} | all-to-all | bytes 851968 | tf_op jit(solution)/shard_map/all_to_all | solution.py:103
  46.2 0.1 bitcast_reduce_fusion
  46.3 16.6 %all-gather = bf16[4,104,256]{2,1,0:T(8,128)(2,1)S(1)} all-gather(bf16[2,104,256]{2,1,0:T(8,128)(2,1)S(1)} %bitcast_reduce_fusion), channel_id=2, replica_groups=mesh['half'=2,'yl'=2,'zl'=8,'zh'=2,'x'=4,'core'=2] {'zh'}, dimensions={0}, use_global_device_ids=true | all-gather | bytes 319488 | tf_op jit(solution)/shard_map/all_gather | solution.py:106
  63.1 15.0 %all_to_all.16 = bf16[8,104,256]{2,1,0:T(8,128)(2,1)S(1)} all-to-all(bf16[8,104,256]{2,1,0:T(8,128)(2,1)S(1)} %pad_maximum_fusion), channel_id=1, replica_groups={{262,260,258,256,6,4,2,0},{263,261,259,257,7,5,3,1},{270,268,266,264,14..., dimensions={0} | all-to-all | bytes 851968 | tf_op jit(solution)/shard_map/all_to_all | solution.py:120
  78.0 4.0 %all_gather.11.left_ref = bf16[1664,256]{1,0:T(8,128)(2,1)S(1)} all-gather(bf16[832,256]{1,0:T(8,128)(2,1)S(1)} %bitcast.44), channel_id=1, replica_groups=mesh['half'=2,'yl'=2,'zl'=8,'zh'=2,'x'=4,'core'=2] {'core'}, dimensions={0}, use_global_device_ids=true | all-gather | bytes 1277952 | tf_op jit(solution)/shard_map/all_gather | solution.py:121
  82.0 1.5 %shard_map.47 = bf16[1664,512]{1,0:T(8,128)(2,1)} custom-call(bf16[1664,256]{1,0:T(8,128)(2,1)S(1)} %all_gather.11.left_ref, bf16[256,512]{1,0:T(8,128)(2,1)S(1)} %bitcast.42), custom_call_target="tpu_custom_call" | custom-call | tf_op jit(solution)/shard_map/pallas_call | solution.py:60
  (5 shorter events, 0.1 us)
Async XLA Ops:
  0.0 16.3 %copy-start = (bf16[1,1664,512]{2,1,0:T(8,128)(2,1)S(1)}, bf16[1,1664,512]{2,1,0:T(8,128)(2,1)}, u32[]{:S(2)}) copy-start(bf16[1,1664,512]{2,1,0:T(8,128)(2,1)} %param.7) | copy-start | bytes 5111812
  1.6 25.5 %all-to-all-start = ((bf16[32,8,512]{2,1,0:T(8,128)(2,1)}), bf16[32,8,512]{2,1,0:T(8,128)(2,1)S(1)}, u32[]{:S(2)}, u32[]{:S(2)}) async-start(bf16[32,8,512]{2,1,0:T(8,128)(2,1)} %shard_map.46), calls=%async_computation | async-start | bytes 524288 | tf_op jit(solution)/shard_map/all_to_all | solution.py:84
  17.3 14.1 %collective-permute-start = (bf16[832,512]{1,0:T(8,128)(2,1)}, bf16[832,512]{1,0:T(8,128)(2,1)S(1)}, u32[]{:S(2)}, u32[]{:S(2)}) collective-permute-start(bf16[832,512]{1,0:T(8,128)(2,1)} %dynamic-slice_bitcast_fusion), channel_id=1, source_target_pairs={{0,1},{1,0},{2,3},{3,2},{4,5},{5,4},{6,7},{7,6},{8,9},{9,8},{10,11... | collective-permute-start | bytes 2555912 | tf_op jit(solution)/shard_map/ppermute | solution.py:91
  27.1 5.0 %collective-permute-start.1 = (bf16[256,512]{1,0:T(8,128)(2,1)S(1)}, bf16[256,512]{1,0:T(8,128)(2,1)S(1)}, u32[]{:S(2)}, u32[]{:S(2)}) collective-permute-start(bf16[256,512]{1,0:T(8,128)(2,1)S(1)} %bitcast.41), channel_id=1, source_target_pairs={{0,1},{1,0},{2,3},{3,2},{4,5},{5,4},{6,7},{7,6},{8,9},{9,8},{10,11... | collective-permute-start | bytes 786440 | tf_op jit(solution)/shard_map/ppermute | solution.py:94

commit v6 on v5

--- a/solution.py
+++ b/solution.py
@@ -80,7 +80,7 @@
         for first in (*range(sections // 2, sections, depth), *range(0, sections // 2, depth))
         for z in range(depth)
     ]
-    owner_order = list(range(owners))[::-1]
+    owner_order = [half * (owners // 2) + x for x in reversed(range(owners // 2)) for half in (1, 0)]
     rows = lax.all_to_all(
         pack(plan, inputs, cotangent, sections), SECTION, 0, 0, axis_index_groups=[order]
     ).reshape(-1, width)
@@ -101,8 +101,8 @@
     partial = near_part.astype(jnp.float32) + far_part.astype(jnp.float32)
     partial = partial.astype(jnp.bfloat16).reshape(owners, -1, row_count)
     gathered = lax.all_to_all(partial, OWNERS, 0, 0, axis_index_groups=[owner_order])
-    gathered = gathered.reshape((2, owners // 2) + gathered.shape[1:])
-    near = jnp.sum(gathered.astype(jnp.float32), axis=1).astype(jnp.bfloat16)
+    gathered = gathered.reshape((owners // 2, 2) + gathered.shape[1:])
+    near = jnp.sum(gathered.astype(jnp.float32), axis=0).astype(jnp.bfloat16)
     both = lax.all_gather(near, "zh")
     total = both[0].astype(jnp.float32) + both[1].astype(jnp.float32)
     pre_sum = total[1]
@@ -111,12 +111,9 @@
     hidden = (pre_sum * logistic).astype(jnp.bfloat16)
     grad_pre = (grad_hidden * logistic * (1.0 + pre_sum * (1.0 - logistic))).astype(jnp.bfloat16)
 
-    answer = jnp.concatenate(
-        [
-            jnp.broadcast_to(hidden[None], (owners // 2,) + hidden.shape),
-            jnp.broadcast_to(grad_pre[None], (owners // 2,) + grad_pre.shape),
-        ]
-    )
+    answer = jnp.stack([hidden, grad_pre])
+    answer = jnp.broadcast_to(answer[None], (owners // 2,) + answer.shape)
+    answer = answer.reshape((owners,) + hidden.shape)
     left = lax.all_to_all(answer, OWNERS, 0, 0, axis_index_groups=[owner_order]).reshape(-1, row_count)
     whole = lax.all_gather(left, "core", axis=0, tiled=True)
     grads = gradient(whole, rows)

time: 83.9 us -> 82.4 us (0.982)
  blocking collectives: 49.2 us -> 47.7 us
    all_to_all x1, blocking collectives: 15 us -> 11.1 us  [local(): lax.all_to_all(answer, OWNERS, 0, 0, axis_index_groups=[owner_order])]
    all_gather x1, blocking collectives: 3.95 us -> 6.35 us  [local(): whole = lax.all_gather(left, 'core', axis=0, tiled=True)]
where the time goes in v6:
time: 82.4 us; the launch traced here: 81.9 us
  blocking collectives  47.7 us (58%)
  starting transfers between devices  21.7 us (26%)
  waiting for transfers between devices  7.36 us (9%)
  Pallas kernels  3.05 us (4%)
  local copies, waits for them, and re-layouts  1 us (1%)
  matrix products  0.83 us (1%)
    all_gather x1, blocking collectives, local(): both = lax.all_gather(near, 'zh')  16.6 us
    all_to_all x1, starting transfers between devices, local(): lax.all_to_all(pack(plan, inputs, cotangent, sections), SECTION, 0, 0, ax...  14.7 us
    all_to_all x1, blocking collectives, local(): lax.all_to_all(partial, OWNERS, 0, 0, axis_index_groups=[owner_order])  13.6 us
    all_to_all x1, blocking collectives, local(): lax.all_to_all(answer, OWNERS, 0, 0, axis_index_groups=[owner_order])  11.1 us
    all_to_all x1, waiting for transfers between devices, local(): lax.all_to_all(pack(plan, inputs, cotangent, sections), SECTION, 0, 0, ax...  6.65 us
    all_gather x1, blocking collectives, local(): whole = lax.all_gather(left, 'core', axis=0, tiled=True)  6.35 us
    ppermute x1, starting transfers between devices, local(): rows_twin = lax.ppermute(rows, 'core', twin)  3.85 us
    ppermute x1, starting transfers between devices, local(): lax.ppermute(lax.dynamic_index_in_dim(piece, 1 - core, 0, keepdims=False)...  3.13 us
  transfers between devices with their start and end apart: 3, of which 2 were waited for; matrix products, arithmetic and copies ran while one was open for 2% of the time, Pallas kernels for 0%

profile of v6, /device:TPU:33, one launch (start us, length us, event | category | flops | bytes accessed | tf_op | source)
XLA Modules:
  0.0 81.9 jit_solution(9305124591820454764)
XLA Ops:
  0.0 0.0 copy-start
  0.0 1.6 %shard_map.46 = bf16[32,8,512]{2,1,0:T(8,128)(2,1)} custom-call(s32[4]{0:T(128)} %plan_ref.1, bf16[4,2,512]{2,1,0:T(2,128)(2,1)} %inputs_ref.1, bf16[4,2,512]{2,1,0:T(2,128)(2,1)} %cotangent_ref.1), custom_call_target="tpu_custom_call" | custom-call | tf_op jit(solution)/shard_map/pallas_call | solution.py:31
  1.6 14.7 %all-to-all-start = ((bf16[32,8,512]{2,1,0:T(8,128)(2,1)}), bf16[32,8,512]{2,1,0:T(8,128)(2,1)S(1)}, u32[]{:S(2)}, u32[]{:S(2)}) async-start(bf16[32,8,512]{2,1,0:T(8,128)(2,1)} %shard_map.46), calls=%async_computation | async-start | bytes 524288 | tf_op jit(solution)/shard_map/all_to_all | solution.py:84
  16.3 0.0 copy-done
  16.3 1.0 %dynamic-slice_bitcast_fusion = bf16[832,512]{1,0:T(8,128)(2,1)} fusion(bf16[2,832,512]{2,1,0:T(8,128)(2,1)S(1)} %bitcast.30, s32[]{:T(128)S(6)} %select_n.8), kind=kLoop, calls=%fused_computation.4 | loop fusion | bytes 1703940 | tf_op jit(solution)/shard_map/jit(dynamic_index_in_dim)/squeeze | solution.py:92
  17.3 3.1 %collective-permute-start = (bf16[832,512]{1,0:T(8,128)(2,1)}, bf16[832,512]{1,0:T(8,128)(2,1)S(1)}, u32[]{:S(2)}, u32[]{:S(2)}) collective-permute-start(bf16[832,512]{1,0:T(8,128)(2,1)} %dynamic-slice_bitcast_fusion), channel_id=1, source_target_pairs={{0,1},{1,0},{2,3},{3,2},{4,5},{5,4},{6,7},{7,6},{8,9},{9,8},{10,11... | collective-permute-start | bytes 2555912 | tf_op jit(solution)/shard_map/ppermute | solution.py:91
  20.4 6.7 %all-to-all-done = bf16[32,8,512]{2,1,0:T(8,128)(2,1)S(1)} async-done(((bf16[32,8,512]{2,1,0:T(8,128)(2,1)}), bf16[32,8,512]{2,1,0:T(8,128)(2,1)S(1)}, u32[]{:S(2)}, u32[]{:S(2)}) %all-to-all-start) | async-done | bytes 262176 | tf_op jit(solution)/shard_map/all_to_all | solution.py:84
  27.1 3.8 %collective-permute-start.1 = (bf16[256,512]{1,0:T(8,128)(2,1)S(1)}, bf16[256,512]{1,0:T(8,128)(2,1)S(1)}, u32[]{:S(2)}, u32[]{:S(2)}) collective-permute-start(bf16[256,512]{1,0:T(8,128)(2,1)S(1)} %bitcast.31), channel_id=1, source_target_pairs={{0,1},{1,0},{2,3},{3,2},{4,5},{5,4},{6,7},{7,6},{8,9},{9,8},{10,11... | collective-permute-start | bytes 786440 | tf_op jit(solution)/shard_map/ppermute | solution.py:94
  30.9 0.4 convolution_convert_fusion.1
  31.3 0.0 collective-permute-done
  31.3 0.7 collective-permute-done.1
  32.0 0.4 convolution_convert_fusion
  32.5 0.1 add_convert_fusion
  32.6 13.6 %all_to_all.15 = bf16[8,104,256]{2,1,0:T(8,128)(2,1)S(1)} all-to-all(bf16[8,104,256]{2,1,0:T(8,128)(2,1)S(1)} %bitcast.33), channel_id=1, replica_groups={{262,6,260,4,258,2,256,0},{263,7,261,5,259,3,257,1},{270,14,268,12,266,..., dimensions={0} | all-to-all | bytes 851968 | tf_op jit(solution)/shard_map/all_to_all | solution.py:103
  46.2 0.1 reduce_sum.12
  46.3 16.6 %all-gather = bf16[4,104,256]{2,1,0:T(8,128)(2,1)S(1)} all-gather(bf16[2,104,256]{2,1,0:T(8,128)(2,1)S(1)} %reduce_sum.12), channel_id=2, replica_groups=mesh['half'=2,'yl'=2,'zl'=8,'zh'=2,'x'=4,'core'=2] {'zh'}, dimensions={0}, use_global_device_ids=true | all-gather | bytes 319488 | tf_op jit(solution)/shard_map/all_gather | solution.py:106
  63.0 11.1 %all_to_all.16 = bf16[8,104,256]{2,1,0:T(8,128)(2,1)S(1)} all-to-all(bf16[8,104,256]{2,1,0:T(8,128)(2,1)S(1)} %bitcast.36), channel_id=1, replica_groups={{262,6,260,4,258,2,256,0},{263,7,261,5,259,3,257,1},{270,14,268,12,266,..., dimensions={0} | all-to-all | bytes 851968 | tf_op jit(solution)/shard_map/all_to_all | solution.py:117
  74.1 6.4 %all_gather.11.left_ref = bf16[1664,256]{1,0:T(8,128)(2,1)S(1)} all-gather(bf16[832,256]{1,0:T(8,128)(2,1)S(1)} %bitcast.34), channel_id=1, replica_groups=mesh['half'=2,'yl'=2,'zl'=8,'zh'=2,'x'=4,'core'=2] {'core'}, dimensions={0}, use_global_device_ids=true | all-gather | bytes 1277952 | tf_op jit(solution)/shard_map/all_gather | solution.py:118
  80.5 1.5 %shard_map.47 = bf16[1664,512]{1,0:T(8,128)(2,1)} custom-call(bf16[1664,256]{1,0:T(8,128)(2,1)S(1)} %all_gather.11.left_ref, bf16[256,512]{1,0:T(8,128)(2,1)S(1)} %bitcast.32), custom_call_target="tpu_custom_call" | custom-call | tf_op jit(solution)/shard_map/pallas_call | solution.py:60
  (4 shorter events, 0.1 us)
Async XLA Ops:
  0.0 16.3 %copy-start = (bf16[1,1664,512]{2,1,0:T(8,128)(2,1)S(1)}, bf16[1,1664,512]{2,1,0:T(8,128)(2,1)}, u32[]{:S(2)}) copy-start(bf16[1,1664,512]{2,1,0:T(8,128)(2,1)} %param.7) | copy-start | bytes 5111812
  1.6 25.5 %all-to-all-start = ((bf16[32,8,512]{2,1,0:T(8,128)(2,1)}), bf16[32,8,512]{2,1,0:T(8,128)(2,1)S(1)}, u32[]{:S(2)}, u32[]{:S(2)}) async-start(bf16[32,8,512]{2,1,0:T(8,128)(2,1)} %shard_map.46), calls=%async_computation | async-start | bytes 524288 | tf_op jit(solution)/shard_map/all_to_all | solution.py:84
  17.3 14.1 %collective-permute-start = (bf16[832,512]{1,0:T(8,128)(2,1)}, bf16[832,512]{1,0:T(8,128)(2,1)S(1)}, u32[]{:S(2)}, u32[]{:S(2)}) collective-permute-start(bf16[832,512]{1,0:T(8,128)(2,1)} %dynamic-slice_bitcast_fusion), channel_id=1, source_target_pairs={{0,1},{1,0},{2,3},{3,2},{4,5},{5,4},{6,7},{7,6},{8,9},{9,8},{10,11... | collective-permute-start | bytes 2555912 | tf_op jit(solution)/shard_map/ppermute | solution.py:91
  27.1 5.0 %collective-permute-start.1 = (bf16[256,512]{1,0:T(8,128)(2,1)S(1)}, bf16[256,512]{1,0:T(8,128)(2,1)S(1)}, u32[]{:S(2)}, u32[]{:S(2)}) collective-permute-start(bf16[256,512]{1,0:T(8,128)(2,1)S(1)} %bitcast.31), channel_id=1, source_target_pairs={{0,1},{1,0},{2,3},{3,2},{4,5},{5,4},{6,7},{7,6},{8,9},{9,8},{10,11... | collective-permute-start | bytes 786440 | tf_op jit(solution)/shard_map/ppermute | solution.py:94

commit v7 on v6

--- a/solution.py
+++ b/solution.py
@@ -87,18 +87,21 @@
     row_count = rows.shape[0]
 
     piece = weights.reshape(2, hidden_units // 2, width)
-    piece_own = lax.dynamic_index_in_dim(piece, core, 0, keepdims=False)
-    piece_twin = lax.ppermute(
-        lax.dynamic_index_in_dim(piece, 1 - core, 0, keepdims=False), "core", twin
+    piece_own, piece_sent = lax.optimization_barrier(
+        (
+            lax.dynamic_index_in_dim(piece, core, 0, keepdims=False),
+            lax.dynamic_index_in_dim(piece, 1 - core, 0, keepdims=False),
+        )
     )
-    rows_twin = lax.ppermute(rows, "core", twin)
+    piece_twin = lax.ppermute(piece_sent, "core", twin)
+    both_rows = lax.all_gather(rows, "core")
+    rows_twin = lax.optimization_barrier(jnp.where(core == 0, both_rows[1], both_rows[0]))
 
     def project(values, matrix):
         return jnp.einsum("fd,rd->fr", matrix, values, preferred_element_type=jnp.float32)
 
-    near_part = lax.optimization_barrier(project(rows, piece_own).astype(jnp.bfloat16))
-    far_part = lax.optimization_barrier(project(rows_twin, piece_twin).astype(jnp.bfloat16))
-    partial = near_part.astype(jnp.float32) + far_part.astype(jnp.float32)
+    pieces = lax.optimization_barrier(jnp.concatenate([piece_own, piece_twin], axis=1))
+    partial = project(jnp.concatenate([rows, rows_twin], axis=1), pieces)
     partial = partial.astype(jnp.bfloat16).reshape(owners, -1, row_count)
     gathered = lax.all_to_all(partial, OWNERS, 0, 0, axis_index_groups=[owner_order])
     gathered = gathered.reshape((owners // 2, 2) + gathered.shape[1:])

time: 82.4 us -> 80.4 us (0.976)
  starting transfers between devices: 21.7 us -> 17.8 us
  blocking collectives: 47.7 us -> 50.7 us
  waiting for transfers between devices: 7.36 us -> 4.71 us
  other arithmetic: 0.26 us -> 1.54 us
    all_to_all x1, waiting for transfers between devices: 6.65 us -> 2.6 us  [local(): lax.all_to_all(pack(plan, inputs, cotangent, sections), SECTION, 0, 0, ax...]
    ppermute x2 -> x1, starting transfers between devices: 6.98 us -> 3.14 us  [local(): piece_twin = lax.ppermute(piece_sent, 'core', twin)]
    all_gather x0 -> x1, blocking collectives: none -> 3.75 us  [local(): both_rows = lax.all_gather(rows, 'core')]
    ppermute x2 -> x1, waiting for transfers between devices: 0.71 us -> 2.11 us  [local(): piece_twin = lax.ppermute(piece_sent, 'core', twin)]
    concatenate x0 -> x1, other arithmetic: none -> 1.36 us  [local(): jnp.concatenate([piece_own, piece_twin], axis=1)]
    all_gather x1, blocking collectives: 16.6 us -> 15.5 us  [local(): both = lax.all_gather(near, 'zh')]
  transfers between devices with their start and end apart: 3 -> 2, of which waited for: 2 -> 2; matrix products, arithmetic and copies ran while one was open for 2% -> 4% of each run, Pallas kernels for 0% -> 0%
where the time goes in v7:
time: 80.4 us; the launch traced here: 80 us
  blocking collectives  50.7 us (63%)
  starting transfers between devices  17.8 us (22%)
  waiting for transfers between devices  4.71 us (6%)
  Pallas kernels  2.94 us (4%)
  local copies, waits for them, and re-layouts  1.56 us (2%)
  other arithmetic  1.54 us (2%)
    all_gather x1, blocking collectives, local(): both = lax.all_gather(near, 'zh')  15.5 us
    all_to_all x1, starting transfers between devices, local(): lax.all_to_all(pack(plan, inputs, cotangent, sections), SECTION, 0, 0, ax...  14.7 us
    all_to_all x1, blocking collectives, local(): lax.all_to_all(partial, OWNERS, 0, 0, axis_index_groups=[owner_order])  13.6 us
    all_to_all x1, blocking collectives, local(): lax.all_to_all(answer, OWNERS, 0, 0, axis_index_groups=[owner_order])  11.6 us
    all_gather x1, blocking collectives, local(): whole = lax.all_gather(left, 'core', axis=0, tiled=True)  6.26 us
    all_gather x1, blocking collectives, local(): both_rows = lax.all_gather(rows, 'core')  3.75 us
    ppermute x1, starting transfers between devices, local(): piece_twin = lax.ppermute(piece_sent, 'core', twin)  3.14 us
    all_to_all x1, waiting for transfers between devices, local(): lax.all_to_all(pack(plan, inputs, cotangent, sections), SECTION, 0, 0, ax...  2.6 us
  transfers between devices with their start and end apart: 2, of which 2 were waited for; matrix products, arithmetic and copies ran while one was open for 4% of the time, Pallas kernels for 0%

profile of v7, /device:TPU:33, one launch (start us, length us, event | category | flops | bytes accessed | tf_op | source)
XLA Modules:
  0.0 80.0 jit_solution(15971444445637163589)
XLA Ops:
  0.0 1.4 %shard_map.46 = bf16[32,8,512]{2,1,0:T(8,128)(2,1)} custom-call(s32[4]{0:T(128)} %plan_ref.1, bf16[4,2,512]{2,1,0:T(2,128)(2,1)} %inputs_ref.1, bf16[4,2,512]{2,1,0:T(2,128)(2,1)} %cotangent_ref.1), custom_call_target="tpu_custom_call" | custom-call | tf_op jit(solution)/shard_map/pallas_call | solution.py:31
  1.5 14.7 %all-to-all-start = ((bf16[32,8,512]{2,1,0:T(8,128)(2,1)}), bf16[32,8,512]{2,1,0:T(8,128)(2,1)S(1)}, u32[]{:S(2)}, u32[]{:S(2)}) async-start(bf16[32,8,512]{2,1,0:T(8,128)(2,1)} %shard_map.46), calls=%async_computation | async-start | bytes 524288 | tf_op jit(solution)/shard_map/all_to_all | solution.py:84
  16.2 1.5 %dynamic-slice_bitcast_fusion = (bf16[832,512]{1,0:T(8,128)(2,1)S(1)}, bf16[832,512]{1,0:T(8,128)(2,1)S(1)}) fusion(bf16[2,832,512]{2,1,0:T(8,128)(2,1)} %bitcast.31, s32[]{:T(128)S(6)} %select_n.19, s32[]{:T(128)S(6)} %select_n.18), kind=kLoop, calls=%fused_computation.2 | loop fusion | bytes 3407880 | tf_op jit(solution)/shard_map/jit(dynamic_index_in_dim)/squeeze | solution.py:93
  17.7 3.1 %collective-permute-start = (bf16[832,512]{1,0:T(8,128)(2,1)S(1)}, bf16[832,512]{1,0:T(8,128)(2,1)}, u32[]{:S(2)}, u32[]{:S(2)}) collective-permute-start(bf16[832,512]{1,0:T(8,128)(2,1)S(1)} %get-tuple-element.8), channel_id=1, source_target_pairs={{0,1},{1,0},{2,3},{3,2},{4,5},{5,4},{6,7},{7,6},{8,9},{9,8},{10,11... | collective-permute-start | bytes 2555912 | tf_op jit(solution)/shard_map/ppermute | solution.py:96
  20.9 2.1 %collective-permute-done = bf16[832,512]{1,0:T(8,128)(2,1)} collective-permute-done((bf16[832,512]{1,0:T(8,128)(2,1)S(1)}, bf16[832,512]{1,0:T(8,128)(2,1)}, u32[]{:S(2)}, u32[]{:S(2)}) %collective-permute-start) | collective-permute-done | bytes 852000 | tf_op jit(solution)/shard_map/ppermute | solution.py:96
  23.0 1.4 %pad_maximum_fusion = bf16[832,1024]{1,0:T(8,128)(2,1)S(1)} fusion(bf16[832,512]{1,0:T(8,128)(2,1)} %collective-permute-done, bf16[832,512]{1,0:T(8,128)(2,1)S(1)} %get-tuple-element.7), kind=kLoop, calls=%fused_computation | loop fusion | flops 3407872 | bytes 3407872 | tf_op jit(solution)/shard_map/concatenate | solution.py:103
  24.3 2.6 %all-to-all-done = bf16[32,8,512]{2,1,0:T(8,128)(2,1)S(1)} async-done(((bf16[32,8,512]{2,1,0:T(8,128)(2,1)}), bf16[32,8,512]{2,1,0:T(8,128)(2,1)S(1)}, u32[]{:S(2)}, u32[]{:S(2)}) %all-to-all-start) | async-done | bytes 262176 | tf_op jit(solution)/shard_map/all_to_all | solution.py:84
  26.9 3.7 %all_gather.12 = bf16[2,256,512]{2,1,0:T(8,128)(2,1)S(1)} all-gather(bf16[1,256,512]{2,1,0:T(8,128)(2,1)S(1)} %bitcast.28), channel_id=1, replica_groups=mesh['half'=2,'yl'=2,'zl'=8,'zh'=2,'x'=4,'core'=2] {'core'}, dimensions={0}, use_global_device_ids=true | all-gather | bytes 786432 | tf_op jit(solution)/shard_map/all_gather | solution.py:97
  30.7 0.6 convolution_convert_fusion
  31.4 13.6 %all_to_all.15 = bf16[8,104,256]{2,1,0:T(8,128)(2,1)S(1)} all-to-all(bf16[8,104,256]{2,1,0:T(8,128)(2,1)S(1)} %bitcast.35), channel_id=1, replica_groups={{262,6,260,4,258,2,256,0},{263,7,261,5,259,3,257,1},{270,14,268,12,266,..., dimensions={0} | all-to-all | bytes 851968 | tf_op jit(solution)/shard_map/all_to_all | solution.py:106
  45.0 0.1 reduce_sum.12
  45.0 15.5 %all-gather = bf16[4,104,256]{2,1,0:T(8,128)(2,1)S(1)} all-gather(bf16[2,104,256]{2,1,0:T(8,128)(2,1)S(1)} %reduce_sum.12), channel_id=2, replica_groups=mesh['half'=2,'yl'=2,'zl'=8,'zh'=2,'x'=4,'core'=2] {'zh'}, dimensions={0}, use_global_device_ids=true | all-gather | bytes 319488 | tf_op jit(solution)/shard_map/all_gather | solution.py:109
  60.6 11.6 %all_to_all.16 = bf16[8,104,256]{2,1,0:T(8,128)(2,1)S(1)} all-to-all(bf16[8,104,256]{2,1,0:T(8,128)(2,1)S(1)} %bitcast.34), channel_id=1, replica_groups={{262,6,260,4,258,2,256,0},{263,7,261,5,259,3,257,1},{270,14,268,12,266,..., dimensions={0} | all-to-all | bytes 851968 | tf_op jit(solution)/shard_map/all_to_all | solution.py:120
  72.3 6.3 %all_gather.15.left_ref = bf16[1664,256]{1,0:T(8,128)(2,1)S(1)} all-gather(bf16[832,256]{1,0:T(8,128)(2,1)S(1)} %bitcast.32), channel_id=1, replica_groups=mesh['half'=2,'yl'=2,'zl'=8,'zh'=2,'x'=4,'core'=2] {'core'}, dimensions={0}, use_global_device_ids=true | all-gather | bytes 1277952 | tf_op jit(solution)/shard_map/all_gather | solution.py:121
  78.5 1.5 %shard_map.47 = bf16[1664,512]{1,0:T(8,128)(2,1)} custom-call(bf16[1664,256]{1,0:T(8,128)(2,1)S(1)} %all_gather.15.left_ref, bf16[256,512]{1,0:T(8,128)(2,1)S(1)} %bitcast.30), custom_call_target="tpu_custom_call" | custom-call | tf_op jit(solution)/shard_map/pallas_call | solution.py:60
  (5 shorter events, 0.1 us)
Async XLA Ops:
  1.5 25.5 %all-to-all-start = ((bf16[32,8,512]{2,1,0:T(8,128)(2,1)}), bf16[32,8,512]{2,1,0:T(8,128)(2,1)S(1)}, u32[]{:S(2)}, u32[]{:S(2)}) async-start(bf16[32,8,512]{2,1,0:T(8,128)(2,1)} %shard_map.46), calls=%async_computation | async-start | bytes 524288 | tf_op jit(solution)/shard_map/all_to_all | solution.py:84
  17.7 5.3 %collective-permute-start = (bf16[832,512]{1,0:T(8,128)(2,1)S(1)}, bf16[832,512]{1,0:T(8,128)(2,1)}, u32[]{:S(2)}, u32[]{:S(2)}) collective-permute-start(bf16[832,512]{1,0:T(8,128)(2,1)S(1)} %get-tuple-element.8), channel_id=1, source_target_pairs={{0,1},{1,0},{2,3},{3,2},{4,5},{5,4},{6,7},{7,6},{8,9},{9,8},{10,11... | collective-permute-start | bytes 2555912 | tf_op jit(solution)/shard_map/ppermute | solution.py:96

commit v8 on v7

--- a/solution.py
+++ b/solution.py
@@ -80,7 +80,7 @@
         for first in (*range(sections // 2, sections, depth), *range(0, sections // 2, depth))
         for z in range(depth)
     ]
-    owner_order = [half * (owners // 2) + x for x in reversed(range(owners // 2)) for half in (1, 0)]
+    owner_order = [half * (owners // 2) + x for x in (3, 1, 2, 0) for half in (1, 0)]
     rows = lax.all_to_all(
         pack(plan, inputs, cotangent, sections), SECTION, 0, 0, axis_index_groups=[order]
     ).reshape(-1, width)

time: 80.4 us -> 80.1 us (level)
  the two profiles are of different devices: /device:TPU:33 before, /device:TPU:185 now
where the time goes in v8:
time: 80.1 us; the launch traced here: 79.7 us
  blocking collectives  55.3 us (69%)
  starting transfers between devices  9.65 us (12%)
  waiting for transfers between devices  8.05 us (10%)
  Pallas kernels  2.94 us (4%)
  local copies, waits for them, and re-layouts  1.56 us (2%)
  other arithmetic  1.54 us (2%)
    all_gather x1, blocking collectives, local(): both = lax.all_gather(near, 'zh')  15.5 us
    all_to_all x1, blocking collectives, local(): lax.all_to_all(partial, OWNERS, 0, 0, axis_index_groups=[owner_order])  15.4 us
    all_to_all x1, blocking collectives, local(): lax.all_to_all(answer, OWNERS, 0, 0, axis_index_groups=[owner_order])  11 us
    all_gather x1, blocking collectives, local(): whole = lax.all_gather(left, 'core', axis=0, tiled=True)  9.8 us
    all_to_all x1, starting transfers between devices, local(): lax.all_to_all(pack(plan, inputs, cotangent, sections), SECTION, 0, 0, ax...  6.51 us
    all_to_all x1, waiting for transfers between devices, local(): lax.all_to_all(pack(plan, inputs, cotangent, sections), SECTION, 0, 0, ax...  5.94 us
    all_gather x1, blocking collectives, local(): both_rows = lax.all_gather(rows, 'core')  3.62 us
    ppermute x1, starting transfers between devices, local(): piece_twin = lax.ppermute(piece_sent, 'core', twin)  3.14 us
  transfers between devices with their start and end apart: 2, of which 2 were waited for; matrix products, arithmetic and copies ran while one was open for 4% of the time, Pallas kernels for 0%

profile of v8, /device:TPU:185, one launch (start us, length us, event | category | flops | bytes accessed | tf_op | source)
XLA Modules:
  0.0 79.7 jit_solution(6729583394768593773)
XLA Ops:
  0.0 1.4 %shard_map.46 = bf16[32,8,512]{2,1,0:T(8,128)(2,1)} custom-call(s32[4]{0:T(128)} %plan_ref.1, bf16[4,2,512]{2,1,0:T(2,128)(2,1)} %inputs_ref.1, bf16[4,2,512]{2,1,0:T(2,128)(2,1)} %cotangent_ref.1), custom_call_target="tpu_custom_call" | custom-call | tf_op jit(solution)/shard_map/pallas_call | solution.py:31
  1.5 6.5 %all-to-all-start = ((bf16[32,8,512]{2,1,0:T(8,128)(2,1)}), bf16[32,8,512]{2,1,0:T(8,128)(2,1)S(1)}, u32[]{:S(2)}, u32[]{:S(2)}) async-start(bf16[32,8,512]{2,1,0:T(8,128)(2,1)} %shard_map.46), calls=%async_computation | async-start | bytes 524288 | tf_op jit(solution)/shard_map/all_to_all | solution.py:84
  8.0 1.5 %dynamic-slice_bitcast_fusion = (bf16[832,512]{1,0:T(8,128)(2,1)S(1)}, bf16[832,512]{1,0:T(8,128)(2,1)S(1)}) fusion(bf16[2,832,512]{2,1,0:T(8,128)(2,1)} %bitcast.31, s32[]{:T(128)S(6)} %select_n.19, s32[]{:T(128)S(6)} %select_n.18), kind=kLoop, calls=%fused_computation.2 | loop fusion | bytes 3407880 | tf_op jit(solution)/shard_map/jit(dynamic_index_in_dim)/squeeze | solution.py:93
  9.5 3.1 %collective-permute-start = (bf16[832,512]{1,0:T(8,128)(2,1)S(1)}, bf16[832,512]{1,0:T(8,128)(2,1)}, u32[]{:S(2)}, u32[]{:S(2)}) collective-permute-start(bf16[832,512]{1,0:T(8,128)(2,1)S(1)} %get-tuple-element.8), channel_id=1, source_target_pairs={{0,1},{1,0},{2,3},{3,2},{4,5},{5,4},{6,7},{7,6},{8,9},{9,8},{10,11... | collective-permute-start | bytes 2555912 | tf_op jit(solution)/shard_map/ppermute | solution.py:96
  12.7 2.1 %collective-permute-done = bf16[832,512]{1,0:T(8,128)(2,1)} collective-permute-done((bf16[832,512]{1,0:T(8,128)(2,1)S(1)}, bf16[832,512]{1,0:T(8,128)(2,1)}, u32[]{:S(2)}, u32[]{:S(2)}) %collective-permute-start) | collective-permute-done | bytes 852000 | tf_op jit(solution)/shard_map/ppermute | solution.py:96
  14.8 1.4 %pad_maximum_fusion = bf16[832,1024]{1,0:T(8,128)(2,1)S(1)} fusion(bf16[832,512]{1,0:T(8,128)(2,1)} %collective-permute-done, bf16[832,512]{1,0:T(8,128)(2,1)S(1)} %get-tuple-element.7), kind=kLoop, calls=%fused_computation | loop fusion | flops 3407872 | bytes 3407872 | tf_op jit(solution)/shard_map/concatenate | solution.py:103
  16.1 5.9 %all-to-all-done = bf16[32,8,512]{2,1,0:T(8,128)(2,1)S(1)} async-done(((bf16[32,8,512]{2,1,0:T(8,128)(2,1)}), bf16[32,8,512]{2,1,0:T(8,128)(2,1)S(1)}, u32[]{:S(2)}, u32[]{:S(2)}) %all-to-all-start) | async-done | bytes 262176 | tf_op jit(solution)/shard_map/all_to_all | solution.py:84
  22.1 3.6 %all_gather.12 = bf16[2,256,512]{2,1,0:T(8,128)(2,1)S(1)} all-gather(bf16[1,256,512]{2,1,0:T(8,128)(2,1)S(1)} %bitcast.28), channel_id=1, replica_groups=mesh['half'=2,'yl'=2,'zl'=8,'zh'=2,'x'=4,'core'=2] {'core'}, dimensions={0}, use_global_device_ids=true | all-gather | bytes 786432 | tf_op jit(solution)/shard_map/all_gather | solution.py:97
  25.7 0.6 convolution_convert_fusion
  26.4 15.4 %all_to_all.15 = bf16[8,104,256]{2,1,0:T(8,128)(2,1)S(1)} all-to-all(bf16[8,104,256]{2,1,0:T(8,128)(2,1)S(1)} %bitcast.35), channel_id=1, replica_groups={{262,6,258,2,260,4,256,0},{263,7,259,3,261,5,257,1},{270,14,266,10,268,..., dimensions={0} | all-to-all | bytes 851968 | tf_op jit(solution)/shard_map/all_to_all | solution.py:106
  41.7 0.1 reduce_sum.12
  41.8 15.5 %all-gather = bf16[4,104,256]{2,1,0:T(8,128)(2,1)S(1)} all-gather(bf16[2,104,256]{2,1,0:T(8,128)(2,1)S(1)} %reduce_sum.12), channel_id=2, replica_groups=mesh['half'=2,'yl'=2,'zl'=8,'zh'=2,'x'=4,'core'=2] {'zh'}, dimensions={0}, use_global_device_ids=true | all-gather | bytes 319488 | tf_op jit(solution)/shard_map/all_gather | solution.py:109
  57.5 11.0 %all_to_all.16 = bf16[8,104,256]{2,1,0:T(8,128)(2,1)S(1)} all-to-all(bf16[8,104,256]{2,1,0:T(8,128)(2,1)S(1)} %bitcast.34), channel_id=1, replica_groups={{262,6,258,2,260,4,256,0},{263,7,259,3,261,5,257,1},{270,14,266,10,268,..., dimensions={0} | all-to-all | bytes 851968 | tf_op jit(solution)/shard_map/all_to_all | solution.py:120
  68.5 9.8 %all_gather.15.left_ref = bf16[1664,256]{1,0:T(8,128)(2,1)S(1)} all-gather(bf16[832,256]{1,0:T(8,128)(2,1)S(1)} %bitcast.32), channel_id=1, replica_groups=mesh['half'=2,'yl'=2,'zl'=8,'zh'=2,'x'=4,'core'=2] {'core'}, dimensions={0}, use_global_device_ids=true | all-gather | bytes 1277952 | tf_op jit(solution)/shard_map/all_gather | solution.py:121
  78.2 1.5 %shard_map.47 = bf16[1664,512]{1,0:T(8,128)(2,1)} custom-call(bf16[1664,256]{1,0:T(8,128)(2,1)S(1)} %all_gather.15.left_ref, bf16[256,512]{1,0:T(8,128)(2,1)S(1)} %bitcast.30), custom_call_target="tpu_custom_call" | custom-call | tf_op jit(solution)/shard_map/pallas_call | solution.py:60
  (5 shorter events, 0.1 us)
Async XLA Ops:
  1.5 20.6 %all-to-all-start = ((bf16[32,8,512]{2,1,0:T(8,128)(2,1)}), bf16[32,8,512]{2,1,0:T(8,128)(2,1)S(1)}, u32[]{:S(2)}, u32[]{:S(2)}) async-start(bf16[32,8,512]{2,1,0:T(8,128)(2,1)} %shard_map.46), calls=%async_computation | async-start | bytes 524288 | tf_op jit(solution)/shard_map/all_to_all | solution.py:84
  9.5 5.3 %collective-permute-start = (bf16[832,512]{1,0:T(8,128)(2,1)S(1)}, bf16[832,512]{1,0:T(8,128)(2,1)}, u32[]{:S(2)}, u32[]{:S(2)}) collective-permute-start(bf16[832,512]{1,0:T(8,128)(2,1)S(1)} %get-tuple-element.8), channel_id=1, source_target_pairs={{0,1},{1,0},{2,3},{3,2},{4,5},{5,4},{6,7},{7,6},{8,9},{9,8},{10,11... | collective-permute-start | bytes 2555912 | tf_op jit(solution)/shard_map/ppermute | solution.py:96

commit v9 on v7

--- a/solution.py
+++ b/solution.py
@@ -9,7 +9,7 @@
 SECTION = ("half", "yl", "zl")
 TENSOR = ("zh", "x", "core")
 OWNERS = ("half", "x")
-TILES = 4
+TILES = 8
 
 
 def pack_kernel(plan_ref, inputs_ref, cotangent_ref, out_ref):
@@ -41,9 +41,9 @@
 
 
 def gradient_kernel(left_ref, rows_ref, out_ref, held_ref, sems):
-    tile = left_ref.shape[0] // 4
+    tile = left_ref.shape[0] // TILES
     copies = []
-    for i in range(4):
+    for i in range(TILES):
         block = pl.ds(i * tile, tile)
         held_ref[block, :] = jnp.dot(
             left_ref[block, :], rows_ref[...], preferred_element_type=jnp.float32
@@ -62,7 +62,7 @@
         out_shape=jax.ShapeDtypeStruct((units, width), left.dtype),
         in_specs=[pl.BlockSpec(memory_space=pltpu.VMEM), pl.BlockSpec(memory_space=pltpu.VMEM)],
         out_specs=pl.BlockSpec(memory_space=pl.ANY),
-        scratch_shapes=[pltpu.VMEM((units, width), left.dtype), pltpu.SemaphoreType.DMA((4,))],
+        scratch_shapes=[pltpu.VMEM((units, width), left.dtype), pltpu.SemaphoreType.DMA((TILES,))],
         compiler_params=pltpu.CompilerParams(vmem_limit_bytes=8 << 20),
     )(left, rows)
 

time: 80.4 us -> 80.4 us (level)
  no operation moved by 1% of the time
where the time goes in v9:
time: 80.4 us; the launch traced here: 80 us
  blocking collectives  50.7 us (63%)
  starting transfers between devices  17.8 us (22%)
  waiting for transfers between devices  4.71 us (6%)
  Pallas kernels  2.92 us (4%)
  local copies, waits for them, and re-layouts  1.56 us (2%)
  other arithmetic  1.54 us (2%)
    all_gather x1, blocking collectives, local(): both = lax.all_gather(near, 'zh')  15.5 us
    all_to_all x1, starting transfers between devices, local(): lax.all_to_all(pack(plan, inputs, cotangent, sections), SECTION, 0, 0, ax...  14.7 us
    all_to_all x1, blocking collectives, local(): lax.all_to_all(partial, OWNERS, 0, 0, axis_index_groups=[owner_order])  13.6 us
    all_to_all x1, blocking collectives, local(): lax.all_to_all(answer, OWNERS, 0, 0, axis_index_groups=[owner_order])  11.6 us
    all_gather x1, blocking collectives, local(): whole = lax.all_gather(left, 'core', axis=0, tiled=True)  6.26 us
    all_gather x1, blocking collectives, local(): both_rows = lax.all_gather(rows, 'core')  3.75 us
    ppermute x1, starting transfers between devices, local(): piece_twin = lax.ppermute(piece_sent, 'core', twin)  3.14 us
    all_to_all x1, waiting for transfers between devices, local(): lax.all_to_all(pack(plan, inputs, cotangent, sections), SECTION, 0, 0, ax...  2.6 us
  transfers between devices with their start and end apart: 2, of which 2 were waited for; matrix products, arithmetic and copies ran while one was open for 4% of the time, Pallas kernels for 0%

profile of v9, /device:TPU:33, one launch (start us, length us, event | category | flops | bytes accessed | tf_op | source)
XLA Modules:
  0.0 80.0 jit_solution(8389834255590784691)
XLA Ops:
  0.0 1.4 %shard_map.46 = bf16[32,8,512]{2,1,0:T(8,128)(2,1)} custom-call(s32[4]{0:T(128)} %plan_ref.1, bf16[4,2,512]{2,1,0:T(2,128)(2,1)} %inputs_ref.1, bf16[4,2,512]{2,1,0:T(2,128)(2,1)} %cotangent_ref.1), custom_call_target="tpu_custom_call" | custom-call | tf_op jit(solution)/shard_map/pallas_call | solution.py:31
  1.5 14.7 %all-to-all-start = ((bf16[32,8,512]{2,1,0:T(8,128)(2,1)}), bf16[32,8,512]{2,1,0:T(8,128)(2,1)S(1)}, u32[]{:S(2)}, u32[]{:S(2)}) async-start(bf16[32,8,512]{2,1,0:T(8,128)(2,1)} %shard_map.46), calls=%async_computation | async-start | bytes 524288 | tf_op jit(solution)/shard_map/all_to_all | solution.py:84
  16.2 1.5 %dynamic-slice_bitcast_fusion = (bf16[832,512]{1,0:T(8,128)(2,1)S(1)}, bf16[832,512]{1,0:T(8,128)(2,1)S(1)}) fusion(bf16[2,832,512]{2,1,0:T(8,128)(2,1)} %bitcast.31, s32[]{:T(128)S(6)} %select_n.19, s32[]{:T(128)S(6)} %select_n.18), kind=kLoop, calls=%fused_computation.2 | loop fusion | bytes 3407880 | tf_op jit(solution)/shard_map/jit(dynamic_index_in_dim)/squeeze | solution.py:93
  17.7 3.1 %collective-permute-start = (bf16[832,512]{1,0:T(8,128)(2,1)S(1)}, bf16[832,512]{1,0:T(8,128)(2,1)}, u32[]{:S(2)}, u32[]{:S(2)}) collective-permute-start(bf16[832,512]{1,0:T(8,128)(2,1)S(1)} %get-tuple-element.8), channel_id=1, source_target_pairs={{0,1},{1,0},{2,3},{3,2},{4,5},{5,4},{6,7},{7,6},{8,9},{9,8},{10,11... | collective-permute-start | bytes 2555912 | tf_op jit(solution)/shard_map/ppermute | solution.py:96
  20.9 2.1 %collective-permute-done = bf16[832,512]{1,0:T(8,128)(2,1)} collective-permute-done((bf16[832,512]{1,0:T(8,128)(2,1)S(1)}, bf16[832,512]{1,0:T(8,128)(2,1)}, u32[]{:S(2)}, u32[]{:S(2)}) %collective-permute-start) | collective-permute-done | bytes 852000 | tf_op jit(solution)/shard_map/ppermute | solution.py:96
  23.0 1.4 %pad_maximum_fusion = bf16[832,1024]{1,0:T(8,128)(2,1)S(1)} fusion(bf16[832,512]{1,0:T(8,128)(2,1)} %collective-permute-done, bf16[832,512]{1,0:T(8,128)(2,1)S(1)} %get-tuple-element.7), kind=kLoop, calls=%fused_computation | loop fusion | flops 3407872 | bytes 3407872 | tf_op jit(solution)/shard_map/concatenate | solution.py:103
  24.3 2.6 %all-to-all-done = bf16[32,8,512]{2,1,0:T(8,128)(2,1)S(1)} async-done(((bf16[32,8,512]{2,1,0:T(8,128)(2,1)}), bf16[32,8,512]{2,1,0:T(8,128)(2,1)S(1)}, u32[]{:S(2)}, u32[]{:S(2)}) %all-to-all-start) | async-done | bytes 262176 | tf_op jit(solution)/shard_map/all_to_all | solution.py:84
  26.9 3.7 %all_gather.12 = bf16[2,256,512]{2,1,0:T(8,128)(2,1)S(1)} all-gather(bf16[1,256,512]{2,1,0:T(8,128)(2,1)S(1)} %bitcast.28), channel_id=1, replica_groups=mesh['half'=2,'yl'=2,'zl'=8,'zh'=2,'x'=4,'core'=2] {'core'}, dimensions={0}, use_global_device_ids=true | all-gather | bytes 786432 | tf_op jit(solution)/shard_map/all_gather | solution.py:97
  30.7 0.6 convolution_convert_fusion
  31.4 13.6 %all_to_all.15 = bf16[8,104,256]{2,1,0:T(8,128)(2,1)S(1)} all-to-all(bf16[8,104,256]{2,1,0:T(8,128)(2,1)S(1)} %bitcast.35), channel_id=1, replica_groups={{262,6,260,4,258,2,256,0},{263,7,261,5,259,3,257,1},{270,14,268,12,266,..., dimensions={0} | all-to-all | bytes 851968 | tf_op jit(solution)/shard_map/all_to_all | solution.py:106
  45.0 0.1 reduce_sum.12
  45.0 15.5 %all-gather = bf16[4,104,256]{2,1,0:T(8,128)(2,1)S(1)} all-gather(bf16[2,104,256]{2,1,0:T(8,128)(2,1)S(1)} %reduce_sum.12), channel_id=2, replica_groups=mesh['half'=2,'yl'=2,'zl'=8,'zh'=2,'x'=4,'core'=2] {'zh'}, dimensions={0}, use_global_device_ids=true | all-gather | bytes 319488 | tf_op jit(solution)/shard_map/all_gather | solution.py:109
  60.6 11.6 %all_to_all.16 = bf16[8,104,256]{2,1,0:T(8,128)(2,1)S(1)} all-to-all(bf16[8,104,256]{2,1,0:T(8,128)(2,1)S(1)} %bitcast.34), channel_id=1, replica_groups={{262,6,260,4,258,2,256,0},{263,7,261,5,259,3,257,1},{270,14,268,12,266,..., dimensions={0} | all-to-all | bytes 851968 | tf_op jit(solution)/shard_map/all_to_all | solution.py:120
  72.3 6.3 %all_gather.15.left_ref = bf16[1664,256]{1,0:T(8,128)(2,1)S(1)} all-gather(bf16[832,256]{1,0:T(8,128)(2,1)S(1)} %bitcast.32), channel_id=1, replica_groups=mesh['half'=2,'yl'=2,'zl'=8,'zh'=2,'x'=4,'core'=2] {'core'}, dimensions={0}, use_global_device_ids=true | all-gather | bytes 1277952 | tf_op jit(solution)/shard_map/all_gather | solution.py:121
  78.5 1.5 %shard_map.47 = bf16[1664,512]{1,0:T(8,128)(2,1)} custom-call(bf16[1664,256]{1,0:T(8,128)(2,1)S(1)} %all_gather.15.left_ref, bf16[256,512]{1,0:T(8,128)(2,1)S(1)} %bitcast.30), custom_call_target="tpu_custom_call" | custom-call | tf_op jit(solution)/shard_map/pallas_call | solution.py:60
  (5 shorter events, 0.1 us)
Async XLA Ops:
  1.5 25.5 %all-to-all-start = ((bf16[32,8,512]{2,1,0:T(8,128)(2,1)}), bf16[32,8,512]{2,1,0:T(8,128)(2,1)S(1)}, u32[]{:S(2)}, u32[]{:S(2)}) async-start(bf16[32,8,512]{2,1,0:T(8,128)(2,1)} %shard_map.46), calls=%async_computation | async-start | bytes 524288 | tf_op jit(solution)/shard_map/all_to_all | solution.py:84
  17.7 5.3 %collective-permute-start = (bf16[832,512]{1,0:T(8,128)(2,1)S(1)}, bf16[832,512]{1,0:T(8,128)(2,1)}, u32[]{:S(2)}, u32[]{:S(2)}) collective-permute-start(bf16[832,512]{1,0:T(8,128)(2,1)S(1)} %get-tuple-element.8), channel_id=1, source_target_pairs={{0,1},{1,0},{2,3},{3,2},{4,5},{5,4},{6,7},{7,6},{8,9},{9,8},{10,11... | collective-permute-start | bytes 2555912 | tf_op jit(solution)/shard_map/ppermute | solution.py:96
